TPU v7x, 32 devices: a whole 2x2x4 slice. The times are simulated.
32 devices in a mesh: dp: 4 (over z), mp: 4 (over y, x), group: 2 (over core).
Axes of the slice: x: 2, y: 2, z: 4, core: 2. Of those that a mesh axis runs over, the one named last changes fastest.
Arguments:
- hidden: bfloat16 [512, 8192], P('dp', 'mp'), may hold values from -6 to 6
- neighbour_ids: int32 [8, 2, 128], P('dp', 'group'), may hold values from 0 to 65535, as said below
- counts: int32 [8], P('dp'), may hold values from 0 to 2
- embed_table: bfloat16 [65536, 8192], P(('dp', 'group'), 'mp'), may hold values from -6 to 6
- w_query: bfloat16 [8192, 4096], P('group', 'mp'), may hold values from -0.0625 to 0.0625
- w_key: bfloat16 [8192, 4096], P('group', 'mp'), may hold values from -0.0625 to 0.0625
- w_value: bfloat16 [8192, 4096], P('group', 'mp'), may hold values from -0.0625 to 0.0625
- w_out: bfloat16 [4096, 8192], P('mp', 'group'), may hold values from -0.09375 to 0.09375
- grad_out: bfloat16 [512, 8192], P('dp', 'mp'), may hold values from -6 to 6
Outputs:
- output: float32 [512, 8192], P('dp', 'mp')
- grad_hidden: float32 [512, 8192], P('dp', 'mp')
- grad_neighbours: float32 [8, 2, 128, 8192], P('dp', 'group', None, 'mp')
Inputs may be any that keep to these rules, and one draw needn't show every extreme that they name: `neighbour_ids`: token ids of the retrieved neighbours; the ids are split into 8 owners of 8192 consecutive ids each; of the 256 ids of one window's neighbour k (blocks of one window, one k), at most 64 belong to one owner, and exactly 64 belong to some owner. neighbours k < counts[c] of block c are used, the others are masked.
All inputs are finite; a program needn't handle non-finite values.
Results may differ from a plain program's by a relative error of at most 0.019.
Values may be sent and summed in bfloat16 or wider, within the bound.
No kernel may reach another device: no remote copies, remote signals or barrier semaphores. Data moves between devices by JAX's collectives and lax.ppermute only.
A program may use at most 256 MiB of HBM per device.

v0:
```python
import math

import jax
import jax.numpy as jnp
from jax import lax
from jax.experimental import pallas as pl
from jax.experimental.pallas import tpu as pltpu
from jax.sharding import PartitionSpec as P

HD = 128
BLOCK = 64
RET = 128
CAP = 64
AXES = ("dp", "mp", "group")


def contract(left, right):
    return lax.dot_general(
        left, right, (((1,), (1,)), ((), ())), preferred_element_type=jnp.float32
    )


def times(left, right):
    return jnp.dot(left, right, preferred_element_type=jnp.float32)


def from_xor(pieces, mask):
    count = pieces.shape[0]
    step = 1
    while step < count:
        split = pieces.reshape(count // (2 * step), 2, step, *pieces.shape[1:])
        swapped = jnp.concatenate([split[:, 1:], split[:, :1]], 1).reshape(pieces.shape)
        pieces = jnp.where((mask & step) != 0, swapped, pieces)
        step *= 2
    return pieces


def params(mib=20):
    return pltpu.CompilerParams(vmem_limit_bytes=mib * 1024 * 1024)


ANY = pl.BlockSpec(memory_space=pl.ANY)
HBM = pl.BlockSpec(memory_space=pltpu.HBM)
SMEM = pl.BlockSpec(memory_space=pltpu.SMEM)
VMEM = pl.BlockSpec(memory_space=pltpu.VMEM)
TILE = 512
COST = pl.CostEstimate(flops=0, bytes_accessed=0, transcendentals=0)


def call(kernel, out_shape, in_specs, name, scratch=(), mib=20):
    return pl.pallas_call(
        kernel,
        out_shape=out_shape,
        in_specs=in_specs,
        out_specs=jax.tree.map(lambda _: VMEM, out_shape),
        scratch_shapes=scratch,
        compiler_params=params(mib),
        cost_estimate=COST,
        name=name,
    )


def tiles(cols):
    tile = min(TILE, cols)
    return [slice(at, at + tile) for at in range(0, cols, tile)]


def load(sources, targets, sems):
    copies = [
        pltpu.make_async_copy(source, target, sems.at[i])
        for i, (source, target) in enumerate(zip(sources, targets))
    ]
    for copy in copies:
        copy.start()
    return lambda i: copies[i].wait()


def pick(weight, chip, there, cols, axis=0):
    size = there.stop - there.start
    rows = pl.ds(pl.multiple_of(chip * cols + there.start, size), size)
    return weight.at[rows] if axis == 0 else weight.at[:, rows]


def pair_scratch(width, depth, cols, extra=()):
    count = 2 * depth // min(TILE, cols)
    return (
        pltpu.VMEM((depth, width), jnp.bfloat16),
        pltpu.VMEM((depth, width), jnp.bfloat16),
        pltpu.SemaphoreType.DMA((count,)),
        *extra,
    )


def load_pair(chips, cols, first, second, first_room, second_room, sems):
    sources, targets, places = [], [], []
    for piece, chip in enumerate(chips):
        for there in tiles(cols):
            room = slice(piece * cols + there.start, piece * cols + there.stop)
            sources += [pick(first, chip, there, cols), pick(second, chip, there, cols)]
            targets += [first_room.at[room], second_room.at[room]]
            places.append((piece, there, room))
    return load(sources, targets, sems), places


def direction_kernel(chips, last, w_key, w_value, _, *refs):
    terms, (key_room, value_room, sems) = refs[:-3], refs[-3:]
    cols = terms[0].shape[1]
    where = [chips[piece] for piece in range(len(terms))]
    wait, places = load_pair(where, cols, w_key, w_value, key_room, value_room, sems)
    heads = terms[0].shape[0] // 2
    width = last.shape[1]
    head = lax.broadcasted_iota(jnp.int32, (heads, width), 0)
    own = head == lax.broadcasted_iota(jnp.int32, (heads, width), 1) // HD
    query = jnp.where(own, last[0:1], 0.0).astype(jnp.bfloat16)
    d_attn = jnp.where(own, last[1:2], 0.0).astype(jnp.bfloat16)
    for i, (piece, there, room) in enumerate(places):
        wait(2 * i)
        wait(2 * i + 1)
        both = [contract(d_attn, value_room[room]), contract(query, key_room[room])]
        terms[piece][:, there] = jnp.concatenate(both, 0).astype(jnp.bfloat16)


def directions(last, chips, w_key, w_value, cols, pieces, after):
    depth, width = w_key.shape
    return call(
        direction_kernel,
        (jax.ShapeDtypeStruct((2 * width // HD, cols), jnp.bfloat16),) * pieces,
        [SMEM, VMEM, HBM, HBM, ANY],
        "directions",
        pair_scratch(width, depth, cols),
        54,
    )(chips, last, w_key, w_value, after)


def settle_kernel(place, *refs):
    first, second = refs[-2:]
    for k in range(place.shape[0]):
        rows = jnp.concatenate([ref[k * CAP : (k + 1) * CAP] for ref in refs[:-3]], 0)
        rows = times(place[k], rows).astype(jnp.bfloat16)
        half = rows.shape[0] // 2
        first[k * half : (k + 1) * half] = rows[:half]
        second[k * half : (k + 1) * half] = rows[half:]


def settle(place, buffers, *after):
    heights = [place.shape[0] * place.shape[1] // 2] * 2
    cols = buffers[0].shape[1]
    tile = min(512, cols)
    return pl.pallas_call(
        settle_kernel,
        out_shape=tuple(jax.ShapeDtypeStruct((h, cols), jnp.bfloat16) for h in heights),
        grid=(cols // tile,),
        in_specs=[pl.BlockSpec(place.shape, lambda t: (0, 0, 0))]
        + [pl.BlockSpec((r.shape[0], tile), lambda t: (0, t)) for r in buffers]
        + [ANY] * len(after),
        out_specs=tuple(pl.BlockSpec((h, tile), lambda t: (0, t)) for h in heights),
        compiler_params=params(),
        cost_estimate=COST,
        name="settle",
    )(place, *buffers, *after)


def gather_terms_kernel(pieces, neighbours, place, *refs):
    mine, passed = refs[pieces:]
    rows = mine.shape[0]
    n_keys = neighbours * rows
    parts = [ref[...].astype(jnp.float32) for ref in refs[:pieces]]
    tokens = parts[-1] + sum(part[n_keys:] for part in parts[:-2])
    total = parts[-2] + sum(part[:n_keys] for part in parts[:-2])
    low, high = total[:rows], total[rows:]
    mine[...] = jnp.where(place[0] == 0, low, high)
    passed[:rows] = jnp.where(place[0] == 0, high, low).astype(jnp.bfloat16)
    passed[rows:] = tokens.astype(jnp.bfloat16)


def gather_terms(pieces, core, neighbours, rows):
    cols = pieces[0].shape[1]
    tile = min(TILE, cols)
    sent = rows + pieces[-1].shape[0]
    return pl.pallas_call(
        lambda *refs: gather_terms_kernel(len(pieces), neighbours, *refs),
        out_shape=(
            jax.ShapeDtypeStruct((rows, cols), jnp.float32),
            jax.ShapeDtypeStruct((sent, cols), jnp.bfloat16),
        ),
        grid=(cols // tile,),
        in_specs=[SMEM] + [pl.BlockSpec((p.shape[0], tile), lambda t: (0, t)) for p in pieces],
        out_specs=(
            pl.BlockSpec((rows, tile), lambda t: (0, t)),
            pl.BlockSpec((sent, tile), lambda t: (0, t)),
        ),
        compiler_params=params(),
        cost_estimate=COST,
        name="gather_terms",
    )(core[None], *pieces)


def finish_kernel(start, mine, passed, other, _, whole, out, hid):
    rows = mine.shape[0]
    whole[0] = mine[...] + other[:rows].astype(jnp.float32)
    both = passed[rows:].astype(jnp.float32) + other[rows:].astype(jnp.float32)
    used = both.shape[0] // 2
    lead = out.shape[0] - used
    valid = lax.broadcasted_iota(jnp.int32, (used, both.shape[1]), 0) + lead >= start
    for which, ref in enumerate((out, hid)):
        ref[:lead] = jnp.zeros((lead, both.shape[1]), jnp.float32)
        ref[lead:] = jnp.where(valid, both[which * used : (which + 1) * used], 0.0)


def finish(mine, passed, other, whole, tokens, start):
    rows, cols = mine.shape
    tile = min(TILE, cols)
    token_spec = pl.BlockSpec((tokens, tile), lambda t: (0, t))
    return pl.pallas_call(
        lambda *refs: finish_kernel(start, *refs),
        out_shape=(jax.ShapeDtypeStruct(whole.shape, whole.dtype),)
        + (jax.ShapeDtypeStruct((tokens, cols), jnp.float32),) * 2,
        grid=(cols // tile,),
        in_specs=[pl.BlockSpec((r.shape[0], tile), lambda t: (0, t)) for r in (mine, passed, other)]
        + [ANY],
        out_specs=(pl.BlockSpec((1, rows, tile), lambda t: (0, 0, t)), token_spec, token_spec),
        input_output_aliases={3: 0},
        compiler_params=params(),
        cost_estimate=COST,
        name="finish",
    )(mine, passed, other, whole)


def along_kernel(dirs, rows, along):
    along[...] = contract(dirs[...], rows[...])


def scores_along(dirs, rows):
    return call(
        along_kernel,
        jax.ShapeDtypeStruct((dirs.shape[0], rows.shape[0]), jnp.float32),
        [VMEM, VMEM],
        "scores_along",
    )(dirs, rows)


def blend_kernel(pieces, heads, place, *refs):
    rows, mixed = refs[pieces : pieces + 2]
    terms = refs[pieces + 2 :]
    along = sum(ref[...] for ref in refs[:pieces])
    all_heads = along.shape[0] // 2
    inv_root = 1.0 / math.sqrt(HD)
    d_prob, score = along[:all_heads], along[all_heads:] * inv_root
    live = lax.broadcasted_iota(jnp.int32, score.shape, 1) // RET < place[0]
    weight = jnp.exp(score) * live.astype(jnp.float32)
    prob = weight / (1.0 + jnp.sum(weight, 1, keepdims=True))
    d_score = prob * (d_prob - jnp.sum(prob * d_prob, 1, keepdims=True))
    both = jnp.concatenate([prob, d_score * inv_root], 0)
    mixed[...] = both
    both = both.astype(jnp.bfloat16)
    line = lax.broadcasted_iota(jnp.int32, (2 * heads, 2 * all_heads), 0)
    column = lax.broadcasted_iota(jnp.int32, (2 * heads, 2 * all_heads), 1)
    line = jnp.where(line < heads, line, line - heads + all_heads)
    for piece, term in enumerate(terms):
        chosen = (line + place[1 + piece] * heads == column).astype(jnp.bfloat16)
        part = times(chosen, both).astype(jnp.bfloat16)
        for there in tiles(rows.shape[1]):
            term[:, there] = times(part, rows[:, there]).astype(jnp.bfloat16)


def blend(along, rows, usable, chips, heads):
    cols = rows.shape[1]
    return call(
        lambda *refs: blend_kernel(len(along), heads, *refs),
        (jax.ShapeDtypeStruct(along[0].shape, jnp.float32),)
        + (jax.ShapeDtypeStruct((2 * heads, cols), jnp.bfloat16),) * chips.shape[0],
        [SMEM] + [VMEM] * (len(along) + 1),
        "blend",
    )(jnp.concatenate([usable[None], chips]), *along, rows)


def second_kernel(core, mixed, dirs, whole):
    rows = whole.shape[1]
    mine = mixed[:, pl.ds(pl.multiple_of(core[0] * rows, HD), rows)]
    whole[0] = times(jnp.transpose(mine).astype(jnp.bfloat16), dirs[...])


def second_grads(core, mixed, dirs):
    cols = dirs.shape[1]
    tile = min(TILE, cols)
    return pl.pallas_call(
        second_kernel,
        out_shape=jax.ShapeDtypeStruct((2, RET, cols), jnp.float32),
        grid=(cols // tile,),
        in_specs=[
            SMEM,
            pl.BlockSpec(mixed.shape, lambda t: (0, 0)),
            pl.BlockSpec((dirs.shape[0], tile), lambda t: (0, t)),
        ],
        out_specs=pl.BlockSpec((1, RET, tile), lambda t: (1, 0, t)),
        compiler_params=params(),
        cost_estimate=COST,
        name="second_grads",
    )(core[None], mixed, dirs)


def stage_kernel(count, *refs):
    wait = load(refs[:count], refs[count + 1 : -1], refs[-1])
    for i in range(count):
        wait(i)


def stage(weights, after):
    count = len(weights)
    return call(
        lambda *refs: stage_kernel(count, *refs),
        tuple(jax.ShapeDtypeStruct(w.shape, w.dtype) for w in weights),
        [HBM] * count + [ANY],
        "stage",
        (pltpu.SemaphoreType.DMA((count,)),),
    )(*weights, after)


def project_kernel(pieces, place, *refs):
    w_key, w_value, mine, other, blend_sums, sums = refs[2 * pieces :]
    n_keys, part = mine.shape[1:]
    first = True
    for piece in range(pieces):
        rows, blends = refs[2 * piece : 2 * piece + 2]
        cols = rows.shape[1]
        for there in tiles(cols):
            size = there.stop - there.start
            here = pl.ds(pl.multiple_of(place[1 + piece] * cols + there.start, size), size)
            both = jnp.concatenate([rows[:, there], blends[:, there]], 0)
            keys, values = times(both, w_key[here]), times(both, w_value[here])
            sums[0] = keys if first else sums[0] + keys
            sums[1] = values if first else sums[1] + values
            first = False
    core = place[0]
    mine[...] = sums[:, :n_keys, pl.ds(pl.multiple_of(core * part, HD), part)]
    other[...] = sums[:, :n_keys, pl.ds(pl.multiple_of((1 - core) * part, HD), part)]
    blend_sums[...] = sums[:, n_keys:]


def project(rows, blends, core, chips, w_key, w_value):
    n_keys, n_blends = rows[0].shape[0], blends[0].shape[0]
    width = w_key.shape[1]
    both = [part for pair in zip(rows, blends) for part in pair]
    half = jax.ShapeDtypeStruct((2, n_keys, width // 2), jnp.float32)
    return call(
        lambda *refs: project_kernel(len(rows), *refs),
        (half, half, jax.ShapeDtypeStruct((2, n_blends, width), jnp.float32)),
        [SMEM] + [VMEM] * (len(both) + 2),
        "project",
        (pltpu.VMEM((2, n_keys + n_blends, width), jnp.float32),),
    )(jnp.concatenate([core[None], chips]), *both, w_key, w_value)


def attend_kernel(place, mine, other, query, d_attn, *refs):
    core, usable = place[0], place[1]
    kv_grads, token_rows = refs[-2:]
    used = query.shape[0]
    n_keys, part = mine.shape[1:]
    inv_root = 1.0 / math.sqrt(HD)
    here = lax.broadcasted_iota(jnp.int32, (used, HD), 0) < used - 1
    key_row = lax.broadcasted_iota(jnp.int32, (n_keys, used), 0) // RET
    key_col = lax.broadcasted_iota(jnp.int32, (used, n_keys), 1) // RET
    live_row = (key_row < usable).astype(jnp.float32)
    live_col = (key_col < usable).astype(jnp.float32)
    for head in range(part // HD):
        cols = slice(head * HD, (head + 1) * HD)
        wide = pl.ds(pl.multiple_of(core * part + head * HD, HD), HD)
        keys = (mine[0, :, cols] + other[0, :, cols]).astype(jnp.bfloat16)
        values = (mine[1, :, cols] + other[1, :, cols]).astype(jnp.bfloat16)
        rows = jnp.where(here, query[:, wide].astype(jnp.float32), 0.0).astype(jnp.bfloat16)
        d_rows = jnp.where(here, d_attn[:, wide].astype(jnp.float32), 0.0)
        d_bf = d_rows.astype(jnp.bfloat16)
        weight = jnp.exp(contract(rows, keys) * inv_root) * live_col
        total = 1.0 + jnp.sum(weight, 1, keepdims=True)
        attn = times(weight.astype(jnp.bfloat16), values) / total
        delta = jnp.sum(d_rows * attn, 1, keepdims=True)
        d_score = (weight / total) * (contract(d_bf, values) - delta)
        d_query = times(d_score.astype(jnp.bfloat16), keys) * inv_root
        turned = jnp.exp(contract(keys, rows) * inv_root) * live_row
        prob = turned / (1.0 + jnp.sum(turned, 0, keepdims=True))
        d_prob = contract(values, d_bf)
        d_turned = prob * (d_prob - jnp.sum(prob * d_prob, 0, keepdims=True))
        d_keys = times(d_turned.astype(jnp.bfloat16), rows) * inv_root
        d_values = times(prob.astype(jnp.bfloat16), d_bf)
        kv_grads[0, :, cols] = d_keys.astype(jnp.bfloat16)
        kv_grads[1, :, cols] = d_values.astype(jnp.bfloat16)
        token_rows[0, :, cols] = attn.astype(jnp.bfloat16)
        token_rows[1, :, cols] = d_query.astype(jnp.bfloat16)


def attend(place, mine, other, query, d_attn):
    used = query.shape[0]
    n_keys, part = mine.shape[1:]
    return pl.pallas_call(
        attend_kernel,
        out_shape=(
            jax.ShapeDtypeStruct((2, n_keys, part), jnp.bfloat16),
            jax.ShapeDtypeStruct((2, used, part), jnp.bfloat16),
        ),
        in_specs=[pl.BlockSpec(memory_space=pltpu.SMEM)]
        + [VMEM] * 4,
        out_specs=(VMEM,) * 2,
        compiler_params=params(),
        cost_estimate=COST,
        name="attend",
    )(place, mine, other, query, d_attn)


def set_halves(core, mine, other, whole):
    part = mine.shape[-1]
    whole[:, :, pl.ds(pl.multiple_of(core * part, HD), part)] = mine[...]
    whole[:, :, pl.ds(pl.multiple_of((1 - core) * part, HD), part)] = other[...]


def term_kernel(place, *refs):
    kv, kv_other, tokens, tokens_other, last, w_key, w_value, w_out, w_query = refs[:9]
    whole, rows, key_room, value_room, sems, out_room, query_room, token_sems = refs[-8:]
    n_keys = kv.shape[1]
    used, width = rows.shape[1:]
    terms, token_terms = refs[10], refs[-9]
    cols = terms.shape[1]
    out_at = token_terms.shape[0] - 2 * used
    hid_at = out_at + used
    chip, core = place[0], place[1]
    wait, places = load_pair([chip], cols, w_key, w_value, key_room, value_room, sems)
    all_cols = slice(0, cols)
    wait_token = load(
        [pick(w_out, chip, all_cols, cols, 1), pick(w_query, chip, all_cols, cols)],
        [out_room, query_room],
        token_sems,
    )
    set_halves(core, kv, kv_other, whole)
    set_halves(core, tokens, tokens_other, rows)
    in_first = lax.broadcasted_iota(jnp.int32, (used, width), 0) < used - 1
    for which in range(2):
        merged = jnp.where(in_first, rows[which].astype(jnp.float32), last[which : which + 1])
        rows[which] = merged.astype(jnp.bfloat16)
    for i, (_, there, room) in enumerate(places):
        wait(2 * i)
        wait(2 * i + 1)
        term = contract(whole[0], key_room[room]) + contract(whole[1], value_room[room])
        terms[:n_keys, there] = term.astype(jnp.bfloat16)
    wait_token(0)
    wait_token(1)
    for there in tiles(cols):
        out_term = times(rows[0], out_room[:, there])
        token_terms[out_at:hid_at, there] = out_term.astype(jnp.bfloat16)
        hid_term = contract(rows[1], query_room[there])
        token_terms[hid_at:, there] = hid_term.astype(jnp.bfloat16)


def head_terms(place, kv, kv_other, tokens, tokens_other, last, weights, cols, after, split):
    n_keys, used, width = kv.shape[1], tokens.shape[1], weights[0].shape[1]
    heights = [n_keys, 2 * used] if split else [n_keys + 2 * used]
    extra = (
        pltpu.VMEM((width, cols), jnp.bfloat16),
        pltpu.VMEM((cols, width), jnp.bfloat16),
        pltpu.SemaphoreType.DMA((2,)),
    )
    return call(
        term_kernel,
        tuple(jax.ShapeDtypeStruct((height, cols), jnp.bfloat16) for height in heights),
        [SMEM] + [VMEM] * 5 + [HBM] * 4 + [ANY],
        "head_terms",
        (
            pltpu.VMEM((2, n_keys, width), jnp.bfloat16),
            pltpu.VMEM((2, used, width), jnp.bfloat16),
            *pair_scratch(width, cols, cols, extra),
        ),
        54,
    )(place, kv, kv_other, tokens, tokens_other, last, *weights, after)


def per_device(
    hidden, neighbour_ids, counts, embed_table, w_query, w_key, w_value, w_out, grad_out
):
    n_dp, n_mp, n_group = (lax.axis_size(name) for name in AXES)
    n_half = n_mp // n_group
    tail_rows = BLOCK - 1
    rows_here = hidden.shape[0]
    cols_here = hidden.shape[1]
    width = w_query.shape[1]
    heads_here = width // HD
    part = width // n_group
    inv_root = 1.0 / math.sqrt(HD)
    block_rows = embed_table.shape[0]
    at_d, at_m, at_g = (lax.axis_index(name) for name in AXES)
    at_y, at_x = at_m // n_half, at_m % n_half

    def move(array, target):
        pairs = []
        for d in range(n_dp):
            for m in range(n_mp):
                for g in range(n_group):
                    to_d, to_m, to_g = target(d, m, g)
                    here = (d * n_mp + m) * n_group + g
                    pairs.append((here, (to_d * n_mp + to_m) * n_group + to_g))
        return lax.ppermute(array, AXES, pairs)

    def to_owner(step_d, step_g):
        return lambda d, m, g: (d ^ step_d, m, g ^ step_g)

    def to_chips(a, b):
        return lambda d, m, g: (d, (g ^ b) * n_half + ((m % n_half) ^ a), m // n_half)

    def to_columns(a, b):
        return lambda d, m, g: (d, g * n_half + ((m % n_half) ^ a), (m // n_half) ^ b)

    def other_core(array):
        return move(array, lambda d, m, g: (d, m, g ^ 1))

    flat_ids = neighbour_ids.reshape(-1)
    slots = flat_ids.shape[0]
    other_ids = other_core(flat_ids)
    pair_ids = jnp.where(
        at_g == 0, jnp.stack([flat_ids, other_ids]), jnp.stack([other_ids, flat_ids])
    )
    every_id = [pair_ids]
    for step in range(1, n_dp):
        every_id.append(move(pair_ids, to_owner(step, 0)))
    every_id = jnp.stack(every_id)
    owner = at_d * n_group + at_g
    local_ids = every_id - owner * block_rows
    inside = (local_ids >= 0) & (local_ids < block_rows)
    before = jnp.triu(jnp.ones((slots, slots), jnp.bfloat16), 1)
    rank = times(inside.astype(jnp.bfloat16).reshape(-1, slots), before)
    rank = rank.reshape(inside.shape).astype(jnp.int32)
    slot_of = jnp.arange(CAP, dtype=jnp.int32)
    chosen = inside[:, :, None, :] & (rank[:, :, None, :] == slot_of[:, None])
    wanted = jnp.sum(jnp.where(chosen, local_ids[:, :, None, :], 0), -1)

    lead = tail_rows // 16 * 16
    used = rows_here - lead
    valid = (jnp.arange(used) + lead >= tail_rows)[:, None]
    hidden, grad_out, other_ids = lax.optimization_barrier((hidden, grad_out, other_ids))
    tokens = jnp.concatenate(
        [jnp.where(valid, hidden[lead:], 0), jnp.where(valid, grad_out[lead:], 0)], 0
    ).astype(jnp.bfloat16)
    token_cols = [move(tokens, to_chips(a, 0)) for a in range(n_half)]
    chips = at_x ^ jnp.arange(n_half, dtype=jnp.int32)
    token_cols = jnp.concatenate(list(from_xor(jnp.stack(token_cols), at_x)), 1)
    query_part = times(token_cols[:used], w_query)
    query_parts = jnp.concatenate([query_part, contract(token_cols[used:], w_out)], 0)
    looked_up = {}
    for step in reversed(range(n_dp)):
        rows = embed_table.at[wanted[step].reshape(-1)].get(mode="promise_in_bounds")
        wanted, looked_up[step] = lax.optimization_barrier((wanted, rows))
    received = {0: looked_up[0]}
    for step in reversed(range(1, n_dp)):
        if n_dp // 2 <= step < n_dp - 1:
            looked_up, received, query_parts = lax.optimization_barrier(
                (looked_up, received, query_parts)
            )
        received[step] = move(looked_up[step], to_owner(step, 0))
    received[0] = looked_up[0]
    buffers = []
    for step in range(n_dp):
        buffers += [received[step], other_core(received[step])]
    own_owner = pair_ids // block_rows
    same = own_owner[:, :, None] == own_owner[:, None, :]
    earlier = jnp.arange(slots)[None, :] < jnp.arange(slots)[:, None]
    own_rank = jnp.sum((same & earlier).astype(jnp.int32), -1)
    sender = jnp.stack(
        [(at_d ^ d) * n_group + (at_g ^ g) for d in range(n_dp) for g in range(n_group)]
    )
    place = (own_owner[:, :, None, None] == sender[:, None]) & (
        own_rank[:, :, None, None] == slot_of
    )
    place = place.astype(jnp.bfloat16).reshape(n_group, slots, -1)

    both = (query_parts + other_core(query_parts)).astype(jnp.bfloat16)
    query, d_attn = both[:used], both[used:]

    head_of = jnp.arange(width)[None, :] // HD
    is_head = head_of == jnp.arange(heads_here)[:, None]
    last = jnp.stack([query[used - 1], d_attn[used - 1]]).astype(jnp.float32)
    dirs = directions(last, chips, w_key, w_value, cols_here, n_half, received[0])
    pieces = [(a, b) for b in range(n_group) for a in range(n_half)]
    all_dirs = jnp.stack([move(dirs[a], to_columns(a, b)) for a, b in pieces])
    all_dirs = from_xor(all_dirs, at_g * n_half + at_x)
    all_dirs = all_dirs.reshape(n_mp, 2, heads_here, cols_here)
    all_dirs = jnp.transpose(all_dirs, (1, 0, 2, 3)).reshape(-1, cols_here)
    rows_first, rows_second = settle(place, buffers, all_dirs)
    first_cols = [move(rows_first, to_chips(a, 0)) for a in range(n_half)]
    along = scores_along(all_dirs, rows_second)
    along = [along] + [
        move(along, lambda d, m, g: (d, m ^ step, g)) for step in range(1, n_mp)
    ]
    mixed, *blends = blend(along, rows_second, counts[1], at_g * n_half + chips, heads_here)
    grads = second_grads(at_g, mixed, all_dirs)
    taken = [move(blends[a], to_chips(a, 0)) for a in range(n_half)]

    staged = stage([w_key, w_value], rows_second)
    kv_mine, kv_other, blend_sums = project(first_cols, taken, at_g, chips, *staged)
    d_query_second = jnp.sum(jnp.where(is_head, blend_sums[0, heads_here:], 0), 0)
    attn_second = jnp.sum(jnp.where(is_head, blend_sums[1, :heads_here], 0), 0)
    second = jnp.stack([attn_second, d_query_second])
    second = second + other_core(second)
    place = jnp.stack([at_g, counts[0]])
    kv_grads, token_rows = attend(place, kv_mine, other_core(kv_other), query, d_attn)
    token_other = other_core(token_rows)
    kv_other = other_core(kv_grads)

    sent = []
    after = second
    for a in reversed(range(n_half)):
        weights = (w_key, w_value, w_out, w_query)
        place = jnp.stack([at_x ^ a, at_g])
        rows = (kv_grads, kv_other, token_rows, token_other, second)
        terms = head_terms(place, *rows, weights, cols_here, after, a == 0)
        sent += [move(term, to_columns(a, 0)) for term in terms]
        after = terms[0]
    mine, passed = gather_terms(sent, at_g, n_group, RET)
    grads, output, grad_hidden = finish(
        mine, passed, other_core(passed), grads, rows_here, tail_rows
    )
    grad_neighbours = grads[:, None]
    return (output, grad_hidden, grad_neighbours)


def solution(mesh):
    return jax.shard_map(
        per_device,
        mesh=mesh,
        in_specs=(
            P("dp", "mp"),
            P("dp", "group", None),
            P("dp"),
            P(("dp", "group"), "mp"),
            P("group", "mp"),
            P("group", "mp"),
            P("group", "mp"),
            P("mp", "group"),
            P("dp", "mp"),
        ),
        out_specs=(P("dp", "mp"), P("dp", "mp"), P("dp", "group", None, "mp")),
        check_vma=False,
    )
```

profile of v0, /device:TPU:0, one launch (start us, length us, event | category | flops | bytes accessed | tf_op | source)
XLA Modules:
  0.0 220.2 jit_solution(5695077964073650741)
XLA Ops:
  4.1 2.9 %collective-permute-start.6 = (bf16[160,2048]{1,0:T(8,128)(2,1)S(1)}, bf16[160,2048]{1,0:T(8,128)(2,1)S(1)}, u32[]{:S(2)}, u32[]{:S(2)}) collective-permute-start(bf16[160,2048]{1,0:T(8,128)(2,1)S(1)} %pad_maximum_fusion.3), channel_id=1, source_target_pairs={{0,2},{1,6},{2,0},{3,4},{4,3},{5,7},{6,1},{7,5},{8,10},{9,14},{10,... | collective-permute-start | bytes 1966088 | tf_op jit(solution)/shard_map/ppermute | solution.py:498
  8.7 2.6 %collective-permute-start.2 = (s32[2,256]{1,0:T(2,128)S(1)}, s32[2,256]{1,0:T(2,128)S(1)}, u32[]{:S(2)}, u32[]{:S(2)}) collective-permute-start(s32[2,256]{1,0:T(2,128)S(1)} %get-tuple-element.87), channel_id=1, source_target_pairs={{0,16},{1,17},{2,18},{3,19},{4,20},{5,21},{6,22},{7,23},{8,24},{9,... | collective-permute-start | bytes 6152 | tf_op jit(solution)/shard_map/ppermute | solution.py:498
  13.2 3.5 %collective-permute-done.3 = s32[2,256]{1,0:T(2,128)S(1)} collective-permute-done((s32[2,256]{1,0:T(2,128)S(1)}, s32[2,256]{1,0:T(2,128)S(1)}, u32[]{:S(2)}, u32[]{:S(2)}) %collective-permute-start.3) | collective-permute-done | bytes 2080 | tf_op jit(solution)/shard_map/ppermute | solution.py:498
  17.2 5.7 %gather_fusion = bf16[128,2048]{1,0:T(8,128)(2,1)} fusion(bf16[8192,2048]{1,0:T(8,128)(2,1)} %param.12, s32[1024]{0:T(1024)S(1)} %pad_clamp_fusion.3), kind=kCustom, calls=%fused_computation | custom fusion | bytes 1049088 | tf_op jit(solution)/shard_map/gather | solution.py:546
  23.0 4.9 %gather_fusion.1 = bf16[128,2048]{1,0:T(8,128)(2,1)S(1)} fusion(bf16[8192,2048]{1,0:T(8,128)(2,1)} %param.12, s32[1024]{0:T(1024)S(1)} %pad_clamp_fusion.2), kind=kCustom, calls=%fused_computation.1 | custom fusion | bytes 1049088 | tf_op jit(solution)/shard_map/gather | solution.py:546
  28.0 5.6 %gather_fusion.2 = bf16[128,2048]{1,0:T(8,128)(2,1)} fusion(bf16[8192,2048]{1,0:T(8,128)(2,1)} %param.12, s32[1024]{0:T(1024)S(1)} %pad_clamp_fusion.1), kind=kCustom, calls=%fused_computation.2 | custom fusion | bytes 1049088 | tf_op jit(solution)/shard_map/gather | solution.py:546
  33.6 5.7 %gather_fusion.3 = bf16[128,2048]{1,0:T(8,128)(2,1)} fusion(bf16[8192,2048]{1,0:T(8,128)(2,1)} %param.12, s32[1024]{0:T(1024)S(1)} %pad_clamp_fusion), kind=kCustom, calls=%fused_computation.3 | custom fusion | bytes 1049088 | tf_op jit(solution)/shard_map/gather | solution.py:546
  40.0 5.1 %fusion.3 = f32[80,1024]{1,0:T(8,128)S(1)} fusion(bf16[4096,1024]{1,0:T(8,128)(2,1)} %refs_8_.3, bf16[160,2048]{1,0:T(8,128)(2,1)S(1)} %get-tuple-element.88, bf16[160,2048]{1,0:T(8,128)(2,1)S(1)} %get-tuple-element.89), kind=kOutput, calls=%fused_computation.13 | convolution fusion | flops 672399360 | bytes 10027008 | tf_op jit(solution)/shard_map/dot_general | solution.py:24
  45.7 2.7 %fusion.5 = f32[80,1024]{1,0:T(8,128)S(1)} fusion(bf16[1024,4096]{1,0:T(8,128)(2,1)S(1)} %bitcast.82, bf16[160,2048]{1,0:T(8,128)(2,1)S(1)} %get-tuple-element.89, bf16[160,2048]{1,0:T(8,128)(2,1)S(1)} %get-tuple-element.88), kind=kOutput, calls=%fused_computation.15 | convolution fusion | flops 672399360 | bytes 10027008 | tf_op jit(solution)/shard_map/dot_general | solution.py:18
  48.5 7.6 %collective-permute-done.4.refs_6_ = bf16[128,2048]{1,0:T(8,128)(2,1)S(1)} collective-permute-done((bf16[128,2048]{1,0:T(8,128)(2,1)}, bf16[128,2048]{1,0:T(8,128)(2,1)S(1)}, u32[]{:S(2)}, u32[]{:S(2)}) %collective-permute-start.4) | collective-permute-done | bytes 524320 | tf_op jit(solution)/shard_map/ppermute | solution.py:498
  57.0 7.3 %collective-permute-start.10 = (bf16[128,2048]{1,0:T(8,128)(2,1)S(1)}, bf16[128,2048]{1,0:T(8,128)(2,1)S(1)}, u32[]{:S(2)}, u32[]{:S(2)}) collective-permute-start(bf16[128,2048]{1,0:T(8,128)(2,1)S(1)} %gather_fusion.1), channel_id=1, source_target_pairs={{0,16},{1,17},{2,18},{3,19},{4,20},{5,21},{6,22},{7,23},{8,24},{9,... | collective-permute-start | bytes 1572872 | tf_op jit(solution)/shard_map/ppermute | solution.py:498
  65.7 8.5 %directions.1 = (bf16[16,2048]{1,0:T(8,128)(2,1)}, bf16[16,2048]{1,0:T(8,128)(2,1)}) custom-call(s32[2]{0:T(128)} %iota_xor_fusion.chips, f32[2,1024]{1,0:T(2,128)} %maximum_convert_fusion.last, bf16[4096,1024]{1,0:T(8,128)(2,1)} %refs_5_.3, bf16[4096,1024]{1,0:T(8,128)(2,1)} %refs_6_.3, bf16[128,2048]{1,0:T(8,128)(2,1)} %gather_fusion.3), custom_call_target="tpu_custom_call" | custom-call | tf_op jit(solution)/shard_map/directions/pallas_call | solution.py:125
  77.3 10.4 %collective-permute-done.10.refs_4_ = bf16[128,2048]{1,0:T(8,128)(2,1)S(1)} collective-permute-done((bf16[128,2048]{1,0:T(8,128)(2,1)S(1)}, bf16[128,2048]{1,0:T(8,128)(2,1)S(1)}, u32[]{:S(2)}, u32[]{:S(2)}) %collective-permute-start.10) | collective-permute-done | bytes 524320 | tf_op jit(solution)/shard_map/ppermute | solution.py:498
  89.5 3.6 %collective-permute-done.17 = bf16[16,2048]{1,0:T(8,128)(2,1)S(1)} collective-permute-done((bf16[16,2048]{1,0:T(8,128)(2,1)}, bf16[16,2048]{1,0:T(8,128)(2,1)S(1)}, u32[]{:S(2)}, u32[]{:S(2)}) %collective-permute-start.17) | collective-permute-done | bytes 65568 | tf_op jit(solution)/shard_map/ppermute | solution.py:498
  104.5 20.8 %collective-permute-done.19.refs_2_ = f32[64,256]{1,0:T(8,128)S(1)} collective-permute-done((f32[64,256]{1,0:T(8,128)S(1)}, f32[64,256]{1,0:T(8,128)S(1)}, u32[]{:S(2)}, u32[]{:S(2)}) %collective-permute-start.19) | collective-permute-done | bytes 65568 | tf_op jit(solution)/shard_map/ppermute | solution.py:498
  129.2 3.4 %copy-done = bf16[4096,1024]{1,0:T(8,128)(2,1)S(1)} copy-done((bf16[4096,1024]{1,0:T(8,128)(2,1)S(1)}, bf16[4096,1024]{1,0:T(8,128)(2,1)}, u32[]{:S(2)}) %copy-start) | copy-done | bytes 8388632
  132.6 3.4 %copy-done.1 = bf16[4096,1024]{1,0:T(8,128)(2,1)S(1)} copy-done((bf16[4096,1024]{1,0:T(8,128)(2,1)S(1)}, bf16[4096,1024]{1,0:T(8,128)(2,1)}, u32[]{:S(2)}) %copy-start.1) | copy-done | bytes 8388632
  137.2 6.4 %project.1 = (f32[2,256,512]{2,1,0:T(8,128)S(1)}, f32[2,256,512]{2,1,0:T(8,128)}, f32[2,16,1024]{2,1,0:T(8,128)S(1)}) custom-call(s32[3]{0:T(128)S(1)} %pad_add_fusion.2.refs_0_, bf16[256,2048]{1,0:T(8,128)(2,1)S(1)} %collective-permute-done.18.refs_1_, bf16[16,2048]{1,0:T(8,128)(2,1)S(1)} %collective-permute-done.22.refs_2_, ...), custom_call_target="tpu_custom_call" | custom-call | tf_op jit(solution)/shard_map/project/pallas_call | solution.py:345
  148.4 3.1 %attend.1 = (bf16[2,256,512]{2,1,0:T(8,128)(2,1)S(1)}, bf16[2,80,512]{2,1,0:T(8,128)(2,1)S(1)}) custom-call(s32[2]{0:T(128)S(1)} %pad_add_fusion.1.place, f32[2,256,512]{2,1,0:T(8,128)S(1)} %get-tuple-element.60.mine, f32[2,256,512]{2,1,0:T(8,128)S(1)} %collective-permute-done.25.other, bf16[80,1024]{1,0:T(8,128)(2,1)S(1)} %get-tuple-element.93.query, ...), custom_call_target="tpu_custom_call" | custom-call | tf_op jit(solution)/shard_map/attend/pallas_call | solution.py:394
  155.6 10.6 %head_terms.2.refs_9_ = bf16[416,2048]{1,0:T(8,128)(2,1)} custom-call(s32[2]{0:T(128)} %pad_add_fusion.place, bf16[2,256,512]{2,1,0:T(8,128)(2,1)} %copy-done.3, bf16[2,256,512]{2,1,0:T(8,128)(2,1)} %copy-done.5, bf16[2,80,512]{2,1,0:T(8,128)(2,1)} %copy-done.4, bf16[2,80,512]{2,1,0:T(8,128)(2,1)} %copy-done.8, f32[2,1024]{1,0:T(2,128)} %fusion.28.refs_4_.refs_9_, ...), custom_call_target="tpu_custom_call" | custom-call | tf_op jit(solution)/shard_map/head_terms/pallas_call | solution.py:460
  168.3 10.2 %head_terms.3 = (bf16[256,2048]{1,0:T(8,128)(2,1)}, bf16[160,2048]{1,0:T(8,128)(2,1)}) custom-call(s32[2]{0:T(128)} %pad_add_fusion.4.place, bf16[2,256,512]{2,1,0:T(8,128)(2,1)} %copy-done.3, bf16[2,256,512]{2,1,0:T(8,128)(2,1)} %copy-done.5, bf16[2,80,512]{2,1,0:T(8,128)(2,1)} %copy-done.4, bf16[2,80,512]{2,1,0:T(8,128)(2,1)} %copy-done.8, ...), custom_call_target="tpu_custom_call" | custom-call | tf_op jit(solution)/shard_map/head_terms/pallas_call | solution.py:460
  182.1 24.4 %collective-permute-done.29.refs_1_ = bf16[416,2048]{1,0:T(8,128)(2,1)S(1)} collective-permute-done((bf16[416,2048]{1,0:T(8,128)(2,1)}, bf16[416,2048]{1,0:T(8,128)(2,1)S(1)}, u32[]{:S(2)}, u32[]{:S(2)}) %collective-permute-start.29) | collective-permute-done | bytes 1703968 | tf_op jit(solution)/shard_map/ppermute | solution.py:498
  207.4 8.0 %collective-permute-start.32 = (bf16[288,2048]{1,0:T(8,128)(2,1)S(1)}, bf16[288,2048]{1,0:T(8,128)(2,1)S(1)}, u32[]{:S(2)}, u32[]{:S(2)}) collective-permute-start(bf16[288,2048]{1,0:T(8,128)(2,1)S(1)} %get-tuple-element.68.refs_1_), channel_id=1, source_target_pairs={{0,1},{1,0},{2,3},{3,2},{4,5},{5,4},{6,7},{7,6},{8,9},{9,8},{10,11... | collective-permute-start | bytes 3538952 | tf_op jit(solution)/shard_map/ppermute | solution.py:498
  217.9 2.3 %finish.1 = (f32[2,128,2048]{2,1,0:T(8,128)}, f32[128,2048]{1,0:T(8,128)}, f32[128,2048]{1,0:T(8,128)}) custom-call(f32[128,2048]{1,0:T(8,128)S(1)} %get-tuple-element.67.refs_0_, bf16[288,2048]{1,0:T(8,128)(2,1)S(1)} %get-tuple-element.68.refs_1_, bf16[288,2048]{1,0:T(8,128)(2,1)S(1)} %collective-permute-done.32.refs_2_, ...), custom_call_target="tpu_custom_call", output_to_operand_aliasing={{0}: (3, {})} | custom-call | tf_op jit(solution)/shard_map/finish/pallas_call | solution.py:214
  (163 shorter events, 50.6 us)
Async XLA Ops:
  3.4 35.9 %collective-permute-start.5 = (bf16[160,2048]{1,0:T(8,128)(2,1)S(1)}, bf16[160,2048]{1,0:T(8,128)(2,1)S(1)}, u32[]{:S(2)}, u32[]{:S(2)}) collective-permute-start(bf16[160,2048]{1,0:T(8,128)(2,1)S(1)} %pad_maximum_fusion.3), channel_id=1, source_target_pairs={{0,0},{1,4},{2,2},{3,6},{4,1},{5,5},{6,3},{7,7},{8,8},{9,12},{10,1... | collective-permute-start | bytes 1966088 | tf_op jit(solution)/shard_map/ppermute | solution.py:498
  4.1 35.2 %collective-permute-start.6 = (bf16[160,2048]{1,0:T(8,128)(2,1)S(1)}, bf16[160,2048]{1,0:T(8,128)(2,1)S(1)}, u32[]{:S(2)}, u32[]{:S(2)}) collective-permute-start(bf16[160,2048]{1,0:T(8,128)(2,1)S(1)} %pad_maximum_fusion.3), channel_id=1, source_target_pairs={{0,2},{1,6},{2,0},{3,4},{4,3},{5,7},{6,1},{7,5},{8,10},{9,14},{10,... | collective-permute-start | bytes 1966088 | tf_op jit(solution)/shard_map/ppermute | solution.py:498
  11.3 5.4 %collective-permute-start.3 = (s32[2,256]{1,0:T(2,128)S(1)}, s32[2,256]{1,0:T(2,128)S(1)}, u32[]{:S(2)}, u32[]{:S(2)}) collective-permute-start(s32[2,256]{1,0:T(2,128)S(1)} %get-tuple-element.87), channel_id=1, source_target_pairs={{0,24},{1,25},{2,26},{3,27},{4,28},{5,29},{6,30},{7,31},{8,16},{9,... | collective-permute-start | bytes 6152 | tf_op jit(solution)/shard_map/ppermute | solution.py:498
  39.3 16.7 %collective-permute-start.4 = (bf16[128,2048]{1,0:T(8,128)(2,1)}, bf16[128,2048]{1,0:T(8,128)(2,1)S(1)}, u32[]{:S(2)}, u32[]{:S(2)}) collective-permute-start(bf16[128,2048]{1,0:T(8,128)(2,1)} %gather_fusion), channel_id=1, source_target_pairs={{0,24},{1,25},{2,26},{3,27},{4,28},{5,29},{6,30},{7,31},{8,16},{9,... | collective-permute-start | bytes 1572872 | tf_op jit(solution)/shard_map/ppermute | solution.py:498
  56.1 8.2 %collective-permute-start.13 = (f32[160,1024]{1,0:T(8,128)S(1)}, f32[160,1024]{1,0:T(8,128)S(1)}, u32[]{:S(2)}, u32[]{:S(2)}) collective-permute-start(f32[160,1024]{1,0:T(8,128)S(1)} %pad_maximum_fusion.4), channel_id=1, source_target_pairs={{0,1},{1,0},{2,3},{3,2},{4,5},{5,4},{6,7},{7,6},{8,9},{9,8},{10,11... | collective-permute-start | bytes 1966088 | tf_op jit(solution)/shard_map/ppermute | solution.py:498
  57.0 30.7 %collective-permute-start.10 = (bf16[128,2048]{1,0:T(8,128)(2,1)S(1)}, bf16[128,2048]{1,0:T(8,128)(2,1)S(1)}, u32[]{:S(2)}, u32[]{:S(2)}) collective-permute-start(bf16[128,2048]{1,0:T(8,128)(2,1)S(1)} %gather_fusion.1), channel_id=1, source_target_pairs={{0,16},{1,17},{2,18},{3,19},{4,20},{5,21},{6,22},{7,23},{8,24},{9,... | collective-permute-start | bytes 1572872 | tf_op jit(solution)/shard_map/ppermute | solution.py:498
  64.3 24.2 %collective-permute-start.8 = (bf16[128,2048]{1,0:T(8,128)(2,1)}, bf16[128,2048]{1,0:T(8,128)(2,1)S(1)}, u32[]{:S(2)}, u32[]{:S(2)}) collective-permute-start(bf16[128,2048]{1,0:T(8,128)(2,1)} %gather_fusion.2), channel_id=1, source_target_pairs={{0,8},{1,9},{2,10},{3,11},{4,12},{5,13},{6,14},{7,15},{8,0},{9,1},... | collective-permute-start | bytes 1572872 | tf_op jit(solution)/shard_map/ppermute | solution.py:498
  74.2 14.3 %collective-permute-start.14 = (bf16[16,2048]{1,0:T(8,128)(2,1)}, bf16[16,2048]{1,0:T(8,128)(2,1)S(1)}, u32[]{:S(2)}, u32[]{:S(2)}) collective-permute-start(bf16[16,2048]{1,0:T(8,128)(2,1)} %get-tuple-element.52), channel_id=1, source_target_pairs={{0,0},{1,4},{2,2},{3,6},{4,1},{5,5},{6,3},{7,7},{8,8},{9,12},{10,1... | collective-permute-start | bytes 196616 | tf_op jit(solution)/shard_map/ppermute | solution.py:498
  75.8 13.2 %collective-permute-start.16 = (bf16[16,2048]{1,0:T(8,128)(2,1)}, bf16[16,2048]{1,0:T(8,128)(2,1)S(1)}, u32[]{:S(2)}, u32[]{:S(2)}) collective-permute-start(bf16[16,2048]{1,0:T(8,128)(2,1)} %get-tuple-element.52), channel_id=1, source_target_pairs={{0,1},{1,5},{2,3},{3,7},{4,0},{5,4},{6,2},{7,6},{8,9},{9,13},{10,1... | collective-permute-start | bytes 196616 | tf_op jit(solution)/shard_map/ppermute | solution.py:498
  77.0 11.9 %collective-permute-start.15 = (bf16[16,2048]{1,0:T(8,128)(2,1)}, bf16[16,2048]{1,0:T(8,128)(2,1)S(1)}, u32[]{:S(2)}, u32[]{:S(2)}) collective-permute-start(bf16[16,2048]{1,0:T(8,128)(2,1)} %get-tuple-element.53), channel_id=1, source_target_pairs={{0,2},{1,6},{2,0},{3,4},{4,3},{5,7},{6,1},{7,5},{8,10},{9,14},{10,... | collective-permute-start | bytes 196616 | tf_op jit(solution)/shard_map/ppermute | solution.py:498
  87.7 5.4 %collective-permute-start.17 = (bf16[16,2048]{1,0:T(8,128)(2,1)}, bf16[16,2048]{1,0:T(8,128)(2,1)S(1)}, u32[]{:S(2)}, u32[]{:S(2)}) collective-permute-start(bf16[16,2048]{1,0:T(8,128)(2,1)} %get-tuple-element.53), channel_id=1, source_target_pairs={{0,3},{1,7},{2,1},{3,5},{4,2},{5,6},{6,0},{7,4},{8,11},{9,15},{10,... | collective-permute-start | bytes 196616 | tf_op jit(solution)/shard_map/ppermute | solution.py:498
  88.4 6.2 %collective-permute-start.7 = (bf16[128,2048]{1,0:T(8,128)(2,1)S(1)}, bf16[128,2048]{1,0:T(8,128)(2,1)S(1)}, u32[]{:S(2)}, u32[]{:S(2)}) collective-permute-start(bf16[128,2048]{1,0:T(8,128)(2,1)S(1)} %copy-done.2), channel_id=1, source_target_pairs={{0,1},{1,0},{2,3},{3,2},{4,5},{5,4},{6,7},{7,6},{8,9},{9,8},{10,11... | collective-permute-start | bytes 1572872 | tf_op jit(solution)/shard_map/ppermute | solution.py:498
  88.5 6.2 %collective-permute-start.12 = (bf16[128,2048]{1,0:T(8,128)(2,1)S(1)}, bf16[128,2048]{1,0:T(8,128)(2,1)S(1)}, u32[]{:S(2)}, u32[]{:S(2)}) collective-permute-start(bf16[128,2048]{1,0:T(8,128)(2,1)S(1)} %collective-permute-done.4.refs_6_), channel_id=1, source_target_pairs={{0,1},{1,0},{2,3},{3,2},{4,5},{5,4},{6,7},{7,6},{8,9},{9,8},{10,11... | collective-permute-start | bytes 1572872 | tf_op jit(solution)/shard_map/ppermute | solution.py:498
  89.0 5.7 %collective-permute-start.11 = (bf16[128,2048]{1,0:T(8,128)(2,1)S(1)}, bf16[128,2048]{1,0:T(8,128)(2,1)S(1)}, u32[]{:S(2)}, u32[]{:S(2)}) collective-permute-start(bf16[128,2048]{1,0:T(8,128)(2,1)S(1)} %collective-permute-done.10.refs_4_), channel_id=1, source_target_pairs={{0,1},{1,0},{2,3},{3,2},{4,5},{5,4},{6,7},{7,6},{8,9},{9,8},{10,11... | collective-permute-start | bytes 1572872 | tf_op jit(solution)/shard_map/ppermute | solution.py:498
  89.0 5.7 %collective-permute-start.9 = (bf16[128,2048]{1,0:T(8,128)(2,1)S(1)}, bf16[128,2048]{1,0:T(8,128)(2,1)S(1)}, u32[]{:S(2)}, u32[]{:S(2)}) collective-permute-start(bf16[128,2048]{1,0:T(8,128)(2,1)S(1)} %collective-permute-done.8.refs_2_), channel_id=1, source_target_pairs={{0,1},{1,0},{2,3},{3,2},{4,5},{5,4},{6,7},{7,6},{8,9},{9,8},{10,11... | collective-permute-start | bytes 1572872 | tf_op jit(solution)/shard_map/ppermute | solution.py:498
  97.0 40.1 %collective-permute-start.18 = (bf16[256,2048]{1,0:T(8,128)(2,1)S(1)}, bf16[256,2048]{1,0:T(8,128)(2,1)S(1)}, u32[]{:S(2)}, u32[]{:S(2)}) collective-permute-start(bf16[256,2048]{1,0:T(8,128)(2,1)S(1)} %get-tuple-element.54), channel_id=1, source_target_pairs={{0,0},{1,4},{2,2},{3,6},{4,1},{5,5},{6,3},{7,7},{8,8},{9,12},{10,1... | collective-permute-start | bytes 3145736 | tf_op jit(solution)/shard_map/ppermute | solution.py:498
  97.7 39.4 %collective-permute-start.23 = (bf16[256,2048]{1,0:T(8,128)(2,1)S(1)}, bf16[256,2048]{1,0:T(8,128)(2,1)S(1)}, u32[]{:S(2)}, u32[]{:S(2)}) collective-permute-start(bf16[256,2048]{1,0:T(8,128)(2,1)S(1)} %get-tuple-element.54), channel_id=1, source_target_pairs={{0,2},{1,6},{2,0},{3,4},{4,3},{5,7},{6,1},{7,5},{8,10},{9,14},{10,... | collective-permute-start | bytes 3145736 | tf_op jit(solution)/shard_map/ppermute | solution.py:498
  99.4 25.9 %collective-permute-start.19 = (f32[64,256]{1,0:T(8,128)S(1)}, f32[64,256]{1,0:T(8,128)S(1)}, u32[]{:S(2)}, u32[]{:S(2)}) collective-permute-start(f32[64,256]{1,0:T(8,128)S(1)} %scores_along.1.refs_1_), channel_id=1, source_target_pairs={{0,2},{1,3},{2,0},{3,1},{4,6},{5,7},{6,4},{7,5},{8,10},{9,11},{10,... | collective-permute-start | bytes 196616 | tf_op jit(solution)/shard_map/ppermute | solution.py:498
  100.9 24.6 %collective-permute-start.20 = (f32[64,256]{1,0:T(8,128)S(1)}, f32[64,256]{1,0:T(8,128)S(1)}, u32[]{:S(2)}, u32[]{:S(2)}) collective-permute-start(f32[64,256]{1,0:T(8,128)S(1)} %scores_along.1.refs_1_), channel_id=1, source_target_pairs={{0,4},{1,5},{2,6},{3,7},{4,0},{5,1},{6,2},{7,3},{8,12},{9,13},{10,... | collective-permute-start | bytes 196616 | tf_op jit(solution)/shard_map/ppermute | solution.py:498
  103.0 22.6 %collective-permute-start.21 = (f32[64,256]{1,0:T(8,128)S(1)}, f32[64,256]{1,0:T(8,128)S(1)}, u32[]{:S(2)}, u32[]{:S(2)}) collective-permute-start(f32[64,256]{1,0:T(8,128)S(1)} %scores_along.1.refs_1_), channel_id=1, source_target_pairs={{0,6},{1,7},{2,4},{3,5},{4,2},{5,3},{6,0},{7,1},{8,14},{9,15},{10,... | collective-permute-start | bytes 196616 | tf_op jit(solution)/shard_map/ppermute | solution.py:498
  126.8 10.3 %collective-permute-start.22 = (bf16[16,2048]{1,0:T(8,128)(2,1)S(1)}, bf16[16,2048]{1,0:T(8,128)(2,1)S(1)}, u32[]{:S(2)}, u32[]{:S(2)}) collective-permute-start(bf16[16,2048]{1,0:T(8,128)(2,1)S(1)} %get-tuple-element.56), channel_id=1, source_target_pairs={{0,0},{1,4},{2,2},{3,6},{4,1},{5,5},{6,3},{7,7},{8,8},{9,12},{10,1... | collective-permute-start | bytes 196616 | tf_op jit(solution)/shard_map/ppermute | solution.py:498
  127.5 9.6 %collective-permute-start.24 = (bf16[16,2048]{1,0:T(8,128)(2,1)S(1)}, bf16[16,2048]{1,0:T(8,128)(2,1)S(1)}, u32[]{:S(2)}, u32[]{:S(2)}) collective-permute-start(bf16[16,2048]{1,0:T(8,128)(2,1)S(1)} %get-tuple-element.57), channel_id=1, source_target_pairs={{0,2},{1,6},{2,0},{3,4},{4,3},{5,7},{6,1},{7,5},{8,10},{9,14},{10,... | collective-permute-start | bytes 196616 | tf_op jit(solution)/shard_map/ppermute | solution.py:498
  166.2 40.3 %collective-permute-start.29 = (bf16[416,2048]{1,0:T(8,128)(2,1)}, bf16[416,2048]{1,0:T(8,128)(2,1)S(1)}, u32[]{:S(2)}, u32[]{:S(2)}) collective-permute-start(bf16[416,2048]{1,0:T(8,128)(2,1)} %head_terms.2.refs_9_), channel_id=1, source_target_pairs={{0,2},{1,6},{2,0},{3,4},{4,3},{5,7},{6,1},{7,5},{8,10},{9,14},{10,... | collective-permute-start | bytes 5111816 | tf_op jit(solution)/shard_map/ppermute | solution.py:498
  207.4 10.5 %collective-permute-start.32 = (bf16[288,2048]{1,0:T(8,128)(2,1)S(1)}, bf16[288,2048]{1,0:T(8,128)(2,1)S(1)}, u32[]{:S(2)}, u32[]{:S(2)}) collective-permute-start(bf16[288,2048]{1,0:T(8,128)(2,1)S(1)} %get-tuple-element.68.refs_1_), channel_id=1, source_target_pairs={{0,1},{1,0},{2,3},{3,2},{4,5},{5,4},{6,7},{7,6},{8,9},{9,8},{10,11... | collective-permute-start | bytes 3538952 | tf_op jit(solution)/shard_map/ppermute | solution.py:498
  (27 other events, 121.3 us)
where the time goes:
time: 221 us; the launch traced here: 220 us
  waiting for transfers between devices  76.2 us (34%)
  Pallas kernels  49.2 us (22%)
  starting transfers between devices  44.3 us (20%)
  local copies, waits for them, and re-layouts  34.3 us (16%)
  matrix products  7.92 us (4%)
  other arithmetic  7.11 us (3%)
    ppermute x33, waiting for transfers between devices, move(): return lax.ppermute(array, AXES, pairs)  76.2 us
    ppermute x33, starting transfers between devices, move(): return lax.ppermute(array, AXES, pairs)  44.3 us
    gather x4, local copies, waits for them, and re-layouts, per_device(): embed_table.at[wanted[step].reshape(-1)].get(mode='promise_in_bounds')  21.8 us
    pallas_call x2, Pallas kernels, head_terms(): call(term_kernel, tuple((jax.ShapeDtypeStruct((height, cols), jnp.bfloat1...  20.8 us
    unnamed x36, local copies, waits for them, and re-layouts  10.9 us
    pallas_call x1, Pallas kernels, directions(): call(direction_kernel, (jax.ShapeDtypeStruct((2 * width // HD, cols), jnp...  8.48 us
    pallas_call x1, Pallas kernels, project(): call(lambda *refs: project_kernel(len(rows), *refs), (half, half, jax.Sha...  6.43 us
    dot_general x2, matrix products, times(): return jnp.dot(left, right, preferred_element_type=jnp.float32)  5.26 us
  transfers between devices with their start and end apart: 33, of which 14 were waited for; matrix products, arithmetic and copies ran while one was open for 17% of the time, Pallas kernels for 11%

commit v1 on v0

--- a/solution.py
+++ b/solution.py
@@ -100,6 +100,52 @@
             targets += [first_room.at[room], second_room.at[room]]
             places.append((piece, there, room))
     return load(sources, targets, sems), places
+
+
+def query_kernel(pieces, chips, *refs):
+    w_query, w_out, sums, query_room, out_room, query_sems, out_sems = refs[pieces:]
+    used = sums.shape[0] // 2
+    cols = refs[0].shape[1]
+    places = [(piece, there) for piece in range(pieces) for there in tiles(cols)]
+    rooms = [
+        slice(piece * cols + there.start, piece * cols + there.stop) for piece, there in places
+    ]
+    wait_query = load(
+        [pick(w_query, chips[piece], there, cols) for piece, there in places],
+        [query_room.at[room] for room in rooms],
+        query_sems,
+    )
+    wait_out = load(
+        [pick(w_out, chips[piece], there, cols, 1) for piece, there in places],
+        [out_room.at[:, room] for room in rooms],
+        out_sems,
+    )
+    for i, ((piece, there), room) in enumerate(zip(places, rooms)):
+        tokens = refs[piece]
+        wait_query(i)
+        query = times(tokens[:used, there], query_room[room])
+        sums[:used] = query if i == 0 else sums[:used] + query
+        wait_out(i)
+        d_attn = contract(tokens[used:, there], out_room[:, room])
+        sums[used:] = d_attn if i == 0 else sums[used:] + d_attn
+
+
+def query_sums(tokens, chips, w_query, w_out):
+    depth, width = w_query.shape
+    count = depth // min(TILE, tokens[0].shape[1])
+    return call(
+        lambda *refs: query_kernel(len(tokens), *refs),
+        jax.ShapeDtypeStruct((tokens[0].shape[0], width), jnp.float32),
+        [SMEM] + [VMEM] * len(tokens) + [HBM, HBM],
+        "query_sums",
+        (
+            pltpu.VMEM((depth, width), jnp.bfloat16),
+            pltpu.VMEM((width, depth), jnp.bfloat16),
+            pltpu.SemaphoreType.DMA((count,)),
+            pltpu.SemaphoreType.DMA((count,)),
+        ),
+        50,
+    )(chips, *tokens, w_query, w_out)
 
 
 def direction_kernel(chips, last, w_key, w_value, _, *refs):
@@ -163,10 +209,8 @@
 def gather_terms_kernel(pieces, neighbours, place, *refs):
     mine, passed = refs[pieces:]
     rows = mine.shape[0]
-    n_keys = neighbours * rows
     parts = [ref[...].astype(jnp.float32) for ref in refs[:pieces]]
-    tokens = parts[-1] + sum(part[n_keys:] for part in parts[:-2])
-    total = parts[-2] + sum(part[:n_keys] for part in parts[:-2])
+    total, tokens = sum(parts[: pieces // 2]), sum(parts[pieces // 2 :])
     low, high = total[:rows], total[rows:]
     mine[...] = jnp.where(place[0] == 0, low, high)
     passed[:rows] = jnp.where(place[0] == 0, high, low).astype(jnp.bfloat16)
@@ -412,63 +456,76 @@
     whole[:, :, pl.ds(pl.multiple_of((1 - core) * part, HD), part)] = other[...]
 
 
-def term_kernel(place, *refs):
-    kv, kv_other, tokens, tokens_other, last, w_key, w_value, w_out, w_query = refs[:9]
-    whole, rows, key_room, value_room, sems, out_room, query_room, token_sems = refs[-8:]
-    n_keys = kv.shape[1]
+def neighbour_kernel(place, *refs):
+    mine, other, w_key, w_value = refs[:4]
+    terms, (whole, key_room, value_room, sems) = refs[4:-4], refs[-4:]
+    cols = terms[0].shape[1]
+    where = [place[1 + piece] for piece in range(len(terms))]
+    wait, places = load_pair(where, cols, w_key, w_value, key_room, value_room, sems)
+    set_halves(place[0], mine, other, whole)
+    for i, (piece, there, room) in enumerate(places):
+        wait(2 * i)
+        wait(2 * i + 1)
+        term = contract(whole[0], key_room[room]) + contract(whole[1], value_room[room])
+        terms[piece][:, there] = term.astype(jnp.bfloat16)
+
+
+def neighbour_terms(core, chips, mine, other, w_key, w_value, cols):
+    n_keys = mine.shape[1]
+    depth, width = w_key.shape
+    return call(
+        neighbour_kernel,
+        (jax.ShapeDtypeStruct((n_keys, cols), jnp.bfloat16),) * chips.shape[0],
+        [SMEM, VMEM, VMEM, HBM, HBM],
+        "neighbour_terms",
+        (pltpu.VMEM((2, n_keys, width), jnp.bfloat16), *pair_scratch(width, depth, cols)),
+        54,
+    )(jnp.concatenate([core[None], chips]), mine, other, w_key, w_value)
+
+
+def token_kernel(place, *refs):
+    mine, other, last, w_out, w_query = refs[:5]
+    terms, (rows, out_room, query_room, sems) = refs[6:-4], refs[-4:]
     used, width = rows.shape[1:]
-    terms, token_terms = refs[10], refs[-9]
-    cols = terms.shape[1]
-    out_at = token_terms.shape[0] - 2 * used
-    hid_at = out_at + used
-    chip, core = place[0], place[1]
-    wait, places = load_pair([chip], cols, w_key, w_value, key_room, value_room, sems)
-    all_cols = slice(0, cols)
-    wait_token = load(
-        [pick(w_out, chip, all_cols, cols, 1), pick(w_query, chip, all_cols, cols)],
-        [out_room, query_room],
-        token_sems,
-    )
-    set_halves(core, kv, kv_other, whole)
-    set_halves(core, tokens, tokens_other, rows)
+    cols = terms[0].shape[1]
+    sources, targets = [], []
+    for piece in range(len(terms)):
+        chip, all_cols = place[1 + piece], slice(0, cols)
+        sources += [pick(w_out, chip, all_cols, cols, 1), pick(w_query, chip, all_cols, cols)]
+        room = slice(piece * cols, (piece + 1) * cols)
+        targets += [out_room.at[:, room], query_room.at[room]]
+    wait = load(sources, targets, sems)
+    set_halves(place[0], mine, other, rows)
     in_first = lax.broadcasted_iota(jnp.int32, (used, width), 0) < used - 1
     for which in range(2):
         merged = jnp.where(in_first, rows[which].astype(jnp.float32), last[which : which + 1])
         rows[which] = merged.astype(jnp.bfloat16)
-    for i, (_, there, room) in enumerate(places):
-        wait(2 * i)
-        wait(2 * i + 1)
-        term = contract(whole[0], key_room[room]) + contract(whole[1], value_room[room])
-        terms[:n_keys, there] = term.astype(jnp.bfloat16)
-    wait_token(0)
-    wait_token(1)
-    for there in tiles(cols):
-        out_term = times(rows[0], out_room[:, there])
-        token_terms[out_at:hid_at, there] = out_term.astype(jnp.bfloat16)
-        hid_term = contract(rows[1], query_room[there])
-        token_terms[hid_at:, there] = hid_term.astype(jnp.bfloat16)
-
-
-def head_terms(place, kv, kv_other, tokens, tokens_other, last, weights, cols, after, split):
-    n_keys, used, width = kv.shape[1], tokens.shape[1], weights[0].shape[1]
-    heights = [n_keys, 2 * used] if split else [n_keys + 2 * used]
-    extra = (
-        pltpu.VMEM((width, cols), jnp.bfloat16),
-        pltpu.VMEM((cols, width), jnp.bfloat16),
-        pltpu.SemaphoreType.DMA((2,)),
-    )
-    return call(
-        term_kernel,
-        tuple(jax.ShapeDtypeStruct((height, cols), jnp.bfloat16) for height in heights),
-        [SMEM] + [VMEM] * 5 + [HBM] * 4 + [ANY],
-        "head_terms",
+    for piece, term in enumerate(terms):
+        wait(2 * piece)
+        wait(2 * piece + 1)
+        for there in tiles(cols):
+            room = slice(piece * cols + there.start, piece * cols + there.stop)
+            term[:used, there] = times(rows[0], out_room[:, room]).astype(jnp.bfloat16)
+            term[used:, there] = contract(rows[1], query_room[room]).astype(jnp.bfloat16)
+
+
+def token_terms(core, chips, mine, other, last, w_out, w_query, cols, after):
+    used = mine.shape[1]
+    depth, width = w_query.shape
+    pieces = chips.shape[0]
+    return call(
+        token_kernel,
+        (jax.ShapeDtypeStruct((2 * used, cols), jnp.bfloat16),) * pieces,
+        [SMEM, VMEM, VMEM, VMEM, HBM, HBM, ANY],
+        "token_terms",
         (
-            pltpu.VMEM((2, n_keys, width), jnp.bfloat16),
             pltpu.VMEM((2, used, width), jnp.bfloat16),
-            *pair_scratch(width, cols, cols, extra),
+            pltpu.VMEM((width, depth), jnp.bfloat16),
+            pltpu.VMEM((depth, width), jnp.bfloat16),
+            pltpu.SemaphoreType.DMA((2 * pieces,)),
         ),
         54,
-    )(place, kv, kv_other, tokens, tokens_other, last, *weights, after)
+    )(jnp.concatenate([core[None], chips]), mine, other, last, w_out, w_query, after)
 
 
 def per_device(
@@ -538,21 +595,21 @@
     ).astype(jnp.bfloat16)
     token_cols = [move(tokens, to_chips(a, 0)) for a in range(n_half)]
     chips = at_x ^ jnp.arange(n_half, dtype=jnp.int32)
-    token_cols = jnp.concatenate(list(from_xor(jnp.stack(token_cols), at_x)), 1)
-    query_part = times(token_cols[:used], w_query)
-    query_parts = jnp.concatenate([query_part, contract(token_cols[used:], w_out)], 0)
+    query_parts = query_sums(token_cols, chips, w_query, w_out)
+    def look_up(step):
+        return embed_table.at[wanted[step].reshape(-1)].get(mode="promise_in_bounds")
+
     looked_up = {}
-    for step in reversed(range(n_dp)):
-        rows = embed_table.at[wanted[step].reshape(-1)].get(mode="promise_in_bounds")
-        wanted, looked_up[step] = lax.optimization_barrier((wanted, rows))
-    received = {0: looked_up[0]}
+    for step in reversed(range(1, n_dp)):
+        wanted, looked_up[step] = lax.optimization_barrier((wanted, look_up(step)))
+    received = {}
     for step in reversed(range(1, n_dp)):
         if n_dp // 2 <= step < n_dp - 1:
-            looked_up, received, query_parts = lax.optimization_barrier(
-                (looked_up, received, query_parts)
+            looked_up, received, query_parts, wanted = lax.optimization_barrier(
+                (looked_up, received, query_parts, wanted)
             )
         received[step] = move(looked_up[step], to_owner(step, 0))
-    received[0] = looked_up[0]
+    received[0] = look_up(0)
     buffers = []
     for step in range(n_dp):
         buffers += [received[step], other_core(received[step])]
@@ -581,11 +638,12 @@
     all_dirs = all_dirs.reshape(n_mp, 2, heads_here, cols_here)
     all_dirs = jnp.transpose(all_dirs, (1, 0, 2, 3)).reshape(-1, cols_here)
     rows_first, rows_second = settle(place, buffers, all_dirs)
-    first_cols = [move(rows_first, to_chips(a, 0)) for a in range(n_half)]
     along = scores_along(all_dirs, rows_second)
     along = [along] + [
         move(along, lambda d, m, g: (d, m ^ step, g)) for step in range(1, n_mp)
     ]
+    rows_first, along = lax.optimization_barrier((rows_first, along))
+    first_cols = [move(rows_first, to_chips(a, 0)) for a in range(n_half)]
     mixed, *blends = blend(along, rows_second, counts[1], at_g * n_half + chips, heads_here)
     grads = second_grads(at_g, mixed, all_dirs)
     taken = [move(blends[a], to_chips(a, 0)) for a in range(n_half)]
@@ -601,15 +659,11 @@
     token_other = other_core(token_rows)
     kv_other = other_core(kv_grads)
 
-    sent = []
-    after = second
-    for a in reversed(range(n_half)):
-        weights = (w_key, w_value, w_out, w_query)
-        place = jnp.stack([at_x ^ a, at_g])
-        rows = (kv_grads, kv_other, token_rows, token_other, second)
-        terms = head_terms(place, *rows, weights, cols_here, after, a == 0)
-        sent += [move(term, to_columns(a, 0)) for term in terms]
-        after = terms[0]
+    neigh = neighbour_terms(at_g, chips, kv_grads, kv_other, w_key, w_value, cols_here)
+    terms = token_terms(
+        at_g, chips, token_rows, token_other, second, w_out, w_query, cols_here, neigh[0]
+    )
+    sent = [move(part[a], to_columns(a, 0)) for part in (neigh, terms) for a in range(n_half)]
     mine, passed = gather_terms(sent, at_g, n_group, RET)
     grads, output, grad_hidden = finish(
         mine, passed, other_core(passed), grads, rows_here, tail_rows

time: 221 us -> 194 us (0.88)
  waiting for transfers between devices: 76.2 us -> 55.5 us
  matrix products: 7.92 us -> 0.14 us
  local copies, waits for them, and re-layouts: 34.3 us -> 27.7 us
  Pallas kernels: 49.2 us -> 54.1 us
    ppermute x33 -> x34, waiting for transfers between devices: 76.2 us -> 55.5 us  [move(): return lax.ppermute(array, AXES, pairs)]
    pallas_call x2 -> x3, Pallas kernels: 20.8 us -> 26.7 us  [the longest x1 9.87 us: token_terms(): call(token_kernel, (jax.ShapeDtypeStruct((2 * used, cols), jnp.bfloat16),...]
    dot_general x2 -> x1, matrix products: 5.26 us -> 0.14 us  [times(): return jnp.dot(left, right, preferred_element_type=jnp.float32)]
    gather x4, local copies, waits for them, and re-layouts: 21.8 us -> 18.1 us  [look_up(): embed_table.at[wanted[step].reshape(-1)].get(mode='promise_in_bounds')]
    dot_general x1 -> x0, matrix products: 2.66 us -> none  [contract(): lax.dot_general(left, right, (((1,), (1,)), ((), ())), preferred_element_...]
    unnamed x36 -> x22, local copies, waits for them, and re-layouts: 10.9 us -> 8.26 us
    ppermute x33 -> x34, starting transfers between devices: 44.3 us -> 46 us  [move(): return lax.ppermute(array, AXES, pairs)]
  transfers between devices with their start and end apart: 33 -> 34, of which waited for: 14 -> 13; matrix products, arithmetic and copies ran while one was open for 17% -> 14% of each run, Pallas kernels for 11% -> 15%
where the time goes in v1:
time: 194 us; the launch traced here: 193 us
  waiting for transfers between devices  55.5 us (29%)
  Pallas kernels  54.1 us (28%)
  starting transfers between devices  46 us (24%)
  local copies, waits for them, and re-layouts  27.7 us (14%)
  other arithmetic  8.43 us (4%)
    ppermute x34, waiting for transfers between devices, move(): return lax.ppermute(array, AXES, pairs)  55.5 us
    ppermute x34, starting transfers between devices, move(): return lax.ppermute(array, AXES, pairs)  46 us
    gather x4, local copies, waits for them, and re-layouts, look_up(): embed_table.at[wanted[step].reshape(-1)].get(mode='promise_in_bounds')  18.1 us
    pallas_call x1, Pallas kernels, token_terms(): call(token_kernel, (jax.ShapeDtypeStruct((2 * used, cols), jnp.bfloat16),...  9.87 us
    pallas_call x1, Pallas kernels, neighbour_terms(): call(neighbour_kernel, (jax.ShapeDtypeStruct((n_keys, cols), jnp.bfloat16...  9.8 us
    pallas_call x1, Pallas kernels, directions(): call(direction_kernel, (jax.ShapeDtypeStruct((2 * width // HD, cols), jnp...  8.4 us
    unnamed x22, local copies, waits for them, and re-layouts  8.26 us
    pallas_call x1, Pallas kernels, query_sums(): call(lambda *refs: query_kernel(len(tokens), *refs), jax.ShapeDtypeStruct...  7.03 us
  transfers between devices with their start and end apart: 34, of which 13 were waited for; matrix products, arithmetic and copies ran while one was open for 14% of the time, Pallas kernels for 15%

profile of v1, /device:TPU:0, one launch (start us, length us, event | category | flops | bytes accessed | tf_op | source)
XLA Modules:
  0.0 193.0 jit_solution(11859913596054529399)
XLA Ops:
  3.0 5.0 %collective-permute-start.3 = (s32[2,256]{1,0:T(2,128)S(1)}, s32[2,256]{1,0:T(2,128)S(1)}, u32[]{:S(2)}, u32[]{:S(2)}) collective-permute-start(s32[2,256]{1,0:T(2,128)S(1)} %get-tuple-element.99), channel_id=1, source_target_pairs={{0,24},{1,25},{2,26},{3,27},{4,28},{5,29},{6,30},{7,31},{8,16},{9,... | collective-permute-start | bytes 6152 | tf_op jit(solution)/shard_map/ppermute | solution.py:555
  13.7 5.7 %gather_fusion = bf16[128,2048]{1,0:T(8,128)(2,1)} fusion(bf16[8192,2048]{1,0:T(8,128)(2,1)} %param.12, s32[1024]{0:T(1024)S(1)} %pad_clamp_fusion.3), kind=kCustom, calls=%fused_computation | custom fusion | bytes 1049088 | tf_op jit(solution)/shard_map/gather | solution.py:600
  19.4 3.6 %collective-permute-start.4 = (bf16[128,2048]{1,0:T(8,128)(2,1)}, bf16[128,2048]{1,0:T(8,128)(2,1)S(1)}, u32[]{:S(2)}, u32[]{:S(2)}) collective-permute-start(bf16[128,2048]{1,0:T(8,128)(2,1)} %gather_fusion), channel_id=1, source_target_pairs={{0,24},{1,25},{2,26},{3,27},{4,28},{5,29},{6,30},{7,31},{8,16},{9,... | collective-permute-start | bytes 1572872 | tf_op jit(solution)/shard_map/ppermute | solution.py:555
  23.1 4.5 %gather_fusion.1 = bf16[128,2048]{1,0:T(8,128)(2,1)} fusion(bf16[8192,2048]{1,0:T(8,128)(2,1)} %param.12, s32[1024]{0:T(1024)S(1)} %pad_clamp_fusion.2), kind=kCustom, calls=%fused_computation.1 | custom fusion | bytes 1049088 | tf_op jit(solution)/shard_map/gather | solution.py:600
  27.7 4.5 %gather_fusion.2 = bf16[128,2048]{1,0:T(8,128)(2,1)} fusion(bf16[8192,2048]{1,0:T(8,128)(2,1)} %param.12, s32[1024]{0:T(1024)S(1)} %pad_clamp_fusion.1), kind=kCustom, calls=%fused_computation.2 | custom fusion | bytes 1049088 | tf_op jit(solution)/shard_map/gather | solution.py:600
  32.1 7.0 %query_sums.1 = f32[160,1024]{1,0:T(8,128)S(1)} custom-call(s32[2]{0:T(128)S(1)} %iota_xor_fusion.refs_0_.chips, bf16[160,2048]{1,0:T(8,128)(2,1)S(1)} %collective-permute-done.5.refs_1_, bf16[160,2048]{1,0:T(8,128)(2,1)S(1)} %collective-permute-done.6.refs_2_, bf16[4096,1024]{1,0:T(8,128)(2,1)} %refs_4_.3, bf16[1024,4096]{1,0:T(8,128)(2,1)} %refs_3_.5), custom_call_target="tpu_custom_call" | custom-call | tf_op jit(solution)/shard_map/query_sums/pallas_call | solution.py:136
  39.2 4.6 %collective-permute-start.13 = (f32[160,1024]{1,0:T(8,128)S(1)}, f32[160,1024]{1,0:T(8,128)S(1)}, u32[]{:S(2)}, u32[]{:S(2)}) collective-permute-start(f32[160,1024]{1,0:T(8,128)S(1)} %query_sums.1), channel_id=1, source_target_pairs={{0,1},{1,0},{2,3},{3,2},{4,5},{5,4},{6,7},{7,6},{8,9},{9,8},{10,11... | collective-permute-start | bytes 1966088 | tf_op jit(solution)/shard_map/ppermute | solution.py:555
  44.2 3.5 %gather_fusion.3 = bf16[128,2048]{1,0:T(8,128)(2,1)} fusion(bf16[8192,2048]{1,0:T(8,128)(2,1)} %param.12, s32[1024]{0:T(1024)S(1)} %pad_clamp_fusion), kind=kCustom, calls=%fused_computation.3 | custom fusion | bytes 1049088 | tf_op jit(solution)/shard_map/gather | solution.py:600
  47.6 5.1 %collective-permute-start.8 = (bf16[128,2048]{1,0:T(8,128)(2,1)}, bf16[128,2048]{1,0:T(8,128)(2,1)S(1)}, u32[]{:S(2)}, u32[]{:S(2)}) collective-permute-start(bf16[128,2048]{1,0:T(8,128)(2,1)} %gather_fusion.2), channel_id=1, source_target_pairs={{0,8},{1,9},{2,10},{3,11},{4,12},{5,13},{6,14},{7,15},{8,0},{9,1},... | collective-permute-start | bytes 1572872 | tf_op jit(solution)/shard_map/ppermute | solution.py:555
  54.5 8.4 %directions.1 = (bf16[16,2048]{1,0:T(8,128)(2,1)}, bf16[16,2048]{1,0:T(8,128)(2,1)}) custom-call(s32[2]{0:T(128)} %copy-done.6, f32[2,1024]{1,0:T(2,128)} %maximum_convert_fusion.last, bf16[4096,1024]{1,0:T(8,128)(2,1)} %refs_2_.1, bf16[4096,1024]{1,0:T(8,128)(2,1)} %refs_3_.4, bf16[128,2048]{1,0:T(8,128)(2,1)} %gather_fusion.3), custom_call_target="tpu_custom_call" | custom-call | tf_op jit(solution)/shard_map/directions/pallas_call | solution.py:171
  66.0 10.2 %collective-permute-done.8.refs_2_ = bf16[128,2048]{1,0:T(8,128)(2,1)S(1)} collective-permute-done((bf16[128,2048]{1,0:T(8,128)(2,1)}, bf16[128,2048]{1,0:T(8,128)(2,1)S(1)}, u32[]{:S(2)}, u32[]{:S(2)}) %collective-permute-start.8) | collective-permute-done | bytes 524320 | tf_op jit(solution)/shard_map/ppermute | solution.py:555
  76.2 2.1 %collective-permute-start.14 = (bf16[16,2048]{1,0:T(8,128)(2,1)}, bf16[16,2048]{1,0:T(8,128)(2,1)}, u32[]{:S(2)}, u32[]{:S(2)}) collective-permute-start(bf16[16,2048]{1,0:T(8,128)(2,1)} %get-tuple-element.57), channel_id=1, source_target_pairs={{0,0},{1,4},{2,2},{3,6},{4,1},{5,5},{6,3},{7,7},{8,8},{9,12},{10,1... | collective-permute-start | bytes 196616 | tf_op jit(solution)/shard_map/ppermute | solution.py:555
  82.9 2.3 %settle.1 = (bf16[256,2048]{1,0:T(8,128)(2,1)S(1)}, bf16[256,2048]{1,0:T(8,128)(2,1)S(1)}) custom-call(bf16[2,256,512]{2,1,0:T(8,128)(2,1)S(1)} %copy.43.place, bf16[128,2048]{1,0:T(8,128)(2,1)S(1)} %copy-done.2, bf16[128,2048]{1,0:T(8,128)(2,1)S(1)} %collective-permute-done.7.refs_1_, bf16[128,2048]{1,0:T(8,128)(2,1)S(1)} %collective-permute-done.8.refs_2_, ...), custom_call_target="tpu_custom_call" | custom-call | tf_op jit(solution)/shard_map/settle/pallas_call | solution.py:195
  99.3 3.4 %copy-done = bf16[4096,1024]{1,0:T(8,128)(2,1)S(1)} copy-done((bf16[4096,1024]{1,0:T(8,128)(2,1)S(1)}, bf16[4096,1024]{1,0:T(8,128)(2,1)}, u32[]{:S(2)}) %copy-start) | copy-done | bytes 8388632
  102.7 3.4 %copy-done.1 = bf16[4096,1024]{1,0:T(8,128)(2,1)S(1)} copy-done((bf16[4096,1024]{1,0:T(8,128)(2,1)S(1)}, bf16[4096,1024]{1,0:T(8,128)(2,1)}, u32[]{:S(2)}) %copy-start.1) | copy-done | bytes 8388632
  107.2 13.6 %collective-permute-done.24.refs_4_ = bf16[16,2048]{1,0:T(8,128)(2,1)S(1)} collective-permute-done((bf16[16,2048]{1,0:T(8,128)(2,1)S(1)}, bf16[16,2048]{1,0:T(8,128)(2,1)S(1)}, u32[]{:S(2)}, u32[]{:S(2)}) %collective-permute-start.24) | collective-permute-done | bytes 65568 | tf_op jit(solution)/shard_map/ppermute | solution.py:555
  120.8 5.5 %project.1 = (f32[2,256,512]{2,1,0:T(8,128)S(1)}, f32[2,256,512]{2,1,0:T(8,128)S(1)}, f32[2,16,1024]{2,1,0:T(8,128)S(1)}) custom-call(s32[3]{0:T(128)S(1)} %pad_add_fusion.refs_0_.place, bf16[256,2048]{1,0:T(8,128)(2,1)S(1)} %collective-permute-done.21.refs_1_, bf16[16,2048]{1,0:T(8,128)(2,1)S(1)} %collective-permute-done.22.refs_2_, ...), custom_call_target="tpu_custom_call" | custom-call | tf_op jit(solution)/shard_map/project/pallas_call | solution.py:389
  129.0 3.1 %attend.1 = (bf16[2,256,512]{2,1,0:T(8,128)(2,1)S(1)}, bf16[2,80,512]{2,1,0:T(8,128)(2,1)S(1)}) custom-call(s32[2]{0:T(128)S(1)} %pad_add_fusion.1.place, f32[2,256,512]{2,1,0:T(8,128)S(1)} %get-tuple-element.70.mine, f32[2,256,512]{2,1,0:T(8,128)S(1)} %collective-permute-done.25.other, bf16[80,1024]{1,0:T(8,128)(2,1)S(1)} %get-tuple-element.101.query, ...), custom_call_target="tpu_custom_call" | custom-call | tf_op jit(solution)/shard_map/attend/pallas_call | solution.py:438
  134.9 9.8 %neighbour_terms.1 = (bf16[256,2048]{1,0:T(8,128)(2,1)}, bf16[256,2048]{1,0:T(8,128)(2,1)}) custom-call(s32[3]{0:T(128)} %copy-done.5, bf16[2,256,512]{2,1,0:T(8,128)(2,1)} %copy-done.3, bf16[2,256,512]{2,1,0:T(8,128)(2,1)} %copy-done.8, bf16[4096,1024]{1,0:T(8,128)(2,1)} %refs_2_.1, bf16[4096,1024]{1,0:T(8,128)(2,1)} %refs_3_.4), custom_call_target="tpu_custom_call" | custom-call | tf_op jit(solution)/shard_map/neighbour_terms/pallas_call | solution.py:476
  148.1 1.9 collective-permute-start.30
  152.2 9.9 %token_terms.1 = (bf16[160,2048]{1,0:T(8,128)(2,1)}, bf16[160,2048]{1,0:T(8,128)(2,1)}) custom-call(s32[3]{0:T(128)} %copy-done.5, bf16[2,80,512]{2,1,0:T(8,128)(2,1)} %copy-done.4, bf16[2,80,512]{2,1,0:T(8,128)(2,1)} %copy-done.9, f32[2,1024]{1,0:T(2,128)} %fusion.19.refs_2_, bf16[1024,4096]{1,0:T(8,128)(2,1)} %refs_3_.5, bf16[4096,1024]{1,0:T(8,128)(2,1)} %refs_4_.3, ...), custom_call_target="tpu_custom_call" | custom-call | tf_op jit(solution)/shard_map/token_terms/pallas_call | solution.py:516
  164.4 21.3 %collective-permute-done.32.refs_4_ = bf16[160,2048]{1,0:T(8,128)(2,1)S(1)} collective-permute-done((bf16[160,2048]{1,0:T(8,128)(2,1)}, bf16[160,2048]{1,0:T(8,128)(2,1)S(1)}, u32[]{:S(2)}, u32[]{:S(2)}) %collective-permute-start.32) | collective-permute-done | bytes 655392 | tf_op jit(solution)/shard_map/ppermute | solution.py:555
  188.3 2.1 %second_grads.1.refs_3_ = f32[2,128,2048]{2,1,0:T(8,128)} custom-call(s32[1]{0:T(128)} %bitcast.refs_0_.core, f32[64,256]{1,0:T(8,128)S(1)} %get-tuple-element.81.mixed, bf16[64,2048]{1,0:T(8,128)(2,1)S(1)} %bitcast.64), custom_call_target="tpu_custom_call" | custom-call | tf_op jit(solution)/shard_map/second_grads/pallas_call | solution.py:330
  190.8 2.3 %finish.1 = (f32[2,128,2048]{2,1,0:T(8,128)}, f32[128,2048]{1,0:T(8,128)}, f32[128,2048]{1,0:T(8,128)}) custom-call(f32[128,2048]{1,0:T(8,128)S(1)} %get-tuple-element.79.refs_0_, bf16[288,2048]{1,0:T(8,128)(2,1)S(1)} %get-tuple-element.80.refs_1_, bf16[288,2048]{1,0:T(8,128)(2,1)S(1)} %collective-permute-done.33.refs_2_, ...), custom_call_target="tpu_custom_call", output_to_operand_aliasing={{0}: (3, {})} | custom-call | tf_op jit(solution)/shard_map/finish/pallas_call | solution.py:258
  (142 shorter events, 49.4 us)
Async XLA Ops:
  3.0 10.2 %collective-permute-start.3 = (s32[2,256]{1,0:T(2,128)S(1)}, s32[2,256]{1,0:T(2,128)S(1)}, u32[]{:S(2)}, u32[]{:S(2)}) collective-permute-start(s32[2,256]{1,0:T(2,128)S(1)} %get-tuple-element.99), channel_id=1, source_target_pairs={{0,24},{1,25},{2,26},{3,27},{4,28},{5,29},{6,30},{7,31},{8,16},{9,... | collective-permute-start | bytes 6152 | tf_op jit(solution)/shard_map/ppermute | solution.py:555
  7.9 5.1 %collective-permute-start.2 = (s32[2,256]{1,0:T(2,128)S(1)}, s32[2,256]{1,0:T(2,128)S(1)}, u32[]{:S(2)}, u32[]{:S(2)}) collective-permute-start(s32[2,256]{1,0:T(2,128)S(1)} %get-tuple-element.99), channel_id=1, source_target_pairs={{0,16},{1,17},{2,18},{3,19},{4,20},{5,21},{6,22},{7,23},{8,24},{9,... | collective-permute-start | bytes 6152 | tf_op jit(solution)/shard_map/ppermute | solution.py:555
  7.9 5.1 %collective-permute-start.1 = (s32[2,256]{1,0:T(2,128)S(1)}, s32[2,256]{1,0:T(2,128)S(1)}, u32[]{:S(2)}, u32[]{:S(2)}) collective-permute-start(s32[2,256]{1,0:T(2,128)S(1)} %get-tuple-element.99), channel_id=1, source_target_pairs={{0,8},{1,9},{2,10},{3,11},{4,12},{5,13},{6,14},{7,15},{8,0},{9,1},... | collective-permute-start | bytes 6152 | tf_op jit(solution)/shard_map/ppermute | solution.py:555
  9.8 22.3 %collective-permute-start.5 = (bf16[160,2048]{1,0:T(8,128)(2,1)S(1)}, bf16[160,2048]{1,0:T(8,128)(2,1)S(1)}, u32[]{:S(2)}, u32[]{:S(2)}) collective-permute-start(bf16[160,2048]{1,0:T(8,128)(2,1)S(1)} %pad_maximum_fusion), channel_id=1, source_target_pairs={{0,0},{1,4},{2,2},{3,6},{4,1},{5,5},{6,3},{7,7},{8,8},{9,12},{10,1... | collective-permute-start | bytes 1966088 | tf_op jit(solution)/shard_map/ppermute | solution.py:555
  10.5 21.6 %collective-permute-start.6 = (bf16[160,2048]{1,0:T(8,128)(2,1)S(1)}, bf16[160,2048]{1,0:T(8,128)(2,1)S(1)}, u32[]{:S(2)}, u32[]{:S(2)}) collective-permute-start(bf16[160,2048]{1,0:T(8,128)(2,1)S(1)} %pad_maximum_fusion), channel_id=1, source_target_pairs={{0,2},{1,6},{2,0},{3,4},{4,3},{5,7},{6,1},{7,5},{8,10},{9,14},{10,... | collective-permute-start | bytes 1966088 | tf_op jit(solution)/shard_map/ppermute | solution.py:555
  19.4 19.7 %collective-permute-start.4 = (bf16[128,2048]{1,0:T(8,128)(2,1)}, bf16[128,2048]{1,0:T(8,128)(2,1)S(1)}, u32[]{:S(2)}, u32[]{:S(2)}) collective-permute-start(bf16[128,2048]{1,0:T(8,128)(2,1)} %gather_fusion), channel_id=1, source_target_pairs={{0,24},{1,25},{2,26},{3,27},{4,28},{5,29},{6,30},{7,31},{8,16},{9,... | collective-permute-start | bytes 1572872 | tf_op jit(solution)/shard_map/ppermute | solution.py:555
  39.2 14.6 %collective-permute-start.13 = (f32[160,1024]{1,0:T(8,128)S(1)}, f32[160,1024]{1,0:T(8,128)S(1)}, u32[]{:S(2)}, u32[]{:S(2)}) collective-permute-start(f32[160,1024]{1,0:T(8,128)S(1)} %query_sums.1), channel_id=1, source_target_pairs={{0,1},{1,0},{2,3},{3,2},{4,5},{5,4},{6,7},{7,6},{8,9},{9,8},{10,11... | collective-permute-start | bytes 1966088 | tf_op jit(solution)/shard_map/ppermute | solution.py:555
  47.6 28.5 %collective-permute-start.8 = (bf16[128,2048]{1,0:T(8,128)(2,1)}, bf16[128,2048]{1,0:T(8,128)(2,1)S(1)}, u32[]{:S(2)}, u32[]{:S(2)}) collective-permute-start(bf16[128,2048]{1,0:T(8,128)(2,1)} %gather_fusion.2), channel_id=1, source_target_pairs={{0,8},{1,9},{2,10},{3,11},{4,12},{5,13},{6,14},{7,15},{8,0},{9,1},... | collective-permute-start | bytes 1572872 | tf_op jit(solution)/shard_map/ppermute | solution.py:555
  52.8 25.9 %collective-permute-start.10 = (bf16[128,2048]{1,0:T(8,128)(2,1)}, bf16[128,2048]{1,0:T(8,128)(2,1)S(1)}, u32[]{:S(2)}, u32[]{:S(2)}) collective-permute-start(bf16[128,2048]{1,0:T(8,128)(2,1)} %gather_fusion.1), channel_id=1, source_target_pairs={{0,16},{1,17},{2,18},{3,19},{4,20},{5,21},{6,22},{7,23},{8,24},{9,... | collective-permute-start | bytes 1572872 | tf_op jit(solution)/shard_map/ppermute | solution.py:555
  62.9 16.1 %collective-permute-start.17 = (bf16[16,2048]{1,0:T(8,128)(2,1)}, bf16[16,2048]{1,0:T(8,128)(2,1)S(1)}, u32[]{:S(2)}, u32[]{:S(2)}) collective-permute-start(bf16[16,2048]{1,0:T(8,128)(2,1)} %get-tuple-element.58), channel_id=1, source_target_pairs={{0,3},{1,7},{2,1},{3,5},{4,2},{5,6},{6,0},{7,4},{8,11},{9,15},{10,... | collective-permute-start | bytes 196616 | tf_op jit(solution)/shard_map/ppermute | solution.py:555
  63.0 16.5 %collective-permute-start.15 = (bf16[16,2048]{1,0:T(8,128)(2,1)}, bf16[16,2048]{1,0:T(8,128)(2,1)}, u32[]{:S(2)}, u32[]{:S(2)}) collective-permute-start(bf16[16,2048]{1,0:T(8,128)(2,1)} %get-tuple-element.58), channel_id=1, source_target_pairs={{0,2},{1,6},{2,0},{3,4},{4,3},{5,7},{6,1},{7,5},{8,10},{9,14},{10,... | collective-permute-start | bytes 196616 | tf_op jit(solution)/shard_map/ppermute | solution.py:555
  64.3 14.9 %collective-permute-start.16 = (bf16[16,2048]{1,0:T(8,128)(2,1)}, bf16[16,2048]{1,0:T(8,128)(2,1)}, u32[]{:S(2)}, u32[]{:S(2)}) collective-permute-start(bf16[16,2048]{1,0:T(8,128)(2,1)} %get-tuple-element.57), channel_id=1, source_target_pairs={{0,1},{1,5},{2,3},{3,7},{4,0},{5,4},{6,2},{7,6},{8,9},{9,13},{10,1... | collective-permute-start | bytes 196616 | tf_op jit(solution)/shard_map/ppermute | solution.py:555
  76.2 3.6 %collective-permute-start.14 = (bf16[16,2048]{1,0:T(8,128)(2,1)}, bf16[16,2048]{1,0:T(8,128)(2,1)}, u32[]{:S(2)}, u32[]{:S(2)}) collective-permute-start(bf16[16,2048]{1,0:T(8,128)(2,1)} %get-tuple-element.57), channel_id=1, source_target_pairs={{0,0},{1,4},{2,2},{3,6},{4,1},{5,5},{6,3},{7,7},{8,8},{9,12},{10,1... | collective-permute-start | bytes 196616 | tf_op jit(solution)/shard_map/ppermute | solution.py:555
  85.6 4.8 %collective-permute-start.18 = (f32[64,256]{1,0:T(8,128)S(1)}, f32[64,256]{1,0:T(8,128)S(1)}, u32[]{:S(2)}, u32[]{:S(2)}) collective-permute-start(f32[64,256]{1,0:T(8,128)S(1)} %scores_along.1.refs_1_), channel_id=1, source_target_pairs={{0,2},{1,3},{2,0},{3,1},{4,6},{5,7},{6,4},{7,5},{8,10},{9,11},{10,... | collective-permute-start | bytes 196616 | tf_op jit(solution)/shard_map/ppermute | solution.py:555
  86.2 5.1 %collective-permute-start.19 = (f32[64,256]{1,0:T(8,128)S(1)}, f32[64,256]{1,0:T(8,128)S(1)}, u32[]{:S(2)}, u32[]{:S(2)}) collective-permute-start(f32[64,256]{1,0:T(8,128)S(1)} %scores_along.1.refs_1_), channel_id=1, source_target_pairs={{0,4},{1,5},{2,6},{3,7},{4,0},{5,1},{6,2},{7,3},{8,12},{9,13},{10,... | collective-permute-start | bytes 196616 | tf_op jit(solution)/shard_map/ppermute | solution.py:555
  87.9 5.2 %collective-permute-start.20 = (f32[64,256]{1,0:T(8,128)S(1)}, f32[64,256]{1,0:T(8,128)S(1)}, u32[]{:S(2)}, u32[]{:S(2)}) collective-permute-start(f32[64,256]{1,0:T(8,128)S(1)} %scores_along.1.refs_1_), channel_id=1, source_target_pairs={{0,6},{1,7},{2,4},{3,5},{4,2},{5,3},{6,0},{7,1},{8,14},{9,15},{10,... | collective-permute-start | bytes 196616 | tf_op jit(solution)/shard_map/ppermute | solution.py:555
  93.1 27.7 %collective-permute-start.21 = (bf16[256,2048]{1,0:T(8,128)(2,1)S(1)}, bf16[256,2048]{1,0:T(8,128)(2,1)S(1)}, u32[]{:S(2)}, u32[]{:S(2)}) collective-permute-start(bf16[256,2048]{1,0:T(8,128)(2,1)S(1)} %get-tuple-element.61), channel_id=1, source_target_pairs={{0,0},{1,4},{2,2},{3,6},{4,1},{5,5},{6,3},{7,7},{8,8},{9,12},{10,1... | collective-permute-start | bytes 3145736 | tf_op jit(solution)/shard_map/ppermute | solution.py:555
  93.8 27.0 %collective-permute-start.23 = (bf16[256,2048]{1,0:T(8,128)(2,1)S(1)}, bf16[256,2048]{1,0:T(8,128)(2,1)S(1)}, u32[]{:S(2)}, u32[]{:S(2)}) collective-permute-start(bf16[256,2048]{1,0:T(8,128)(2,1)S(1)} %get-tuple-element.61), channel_id=1, source_target_pairs={{0,2},{1,6},{2,0},{3,4},{4,3},{5,7},{6,1},{7,5},{8,10},{9,14},{10,... | collective-permute-start | bytes 3145736 | tf_op jit(solution)/shard_map/ppermute | solution.py:555
  97.9 9.3 %collective-permute-start.22 = (bf16[16,2048]{1,0:T(8,128)(2,1)S(1)}, bf16[16,2048]{1,0:T(8,128)(2,1)S(1)}, u32[]{:S(2)}, u32[]{:S(2)}) collective-permute-start(bf16[16,2048]{1,0:T(8,128)(2,1)S(1)} %get-tuple-element.66), channel_id=1, source_target_pairs={{0,0},{1,4},{2,2},{3,6},{4,1},{5,5},{6,3},{7,7},{8,8},{9,12},{10,1... | collective-permute-start | bytes 196616 | tf_op jit(solution)/shard_map/ppermute | solution.py:555
  98.6 22.2 %collective-permute-start.24 = (bf16[16,2048]{1,0:T(8,128)(2,1)S(1)}, bf16[16,2048]{1,0:T(8,128)(2,1)S(1)}, u32[]{:S(2)}, u32[]{:S(2)}) collective-permute-start(bf16[16,2048]{1,0:T(8,128)(2,1)S(1)} %get-tuple-element.67), channel_id=1, source_target_pairs={{0,2},{1,6},{2,0},{3,4},{4,3},{5,7},{6,1},{7,5},{8,10},{9,14},{10,... | collective-permute-start | bytes 196616 | tf_op jit(solution)/shard_map/ppermute | solution.py:555
  144.7 40.9 %collective-permute-start.27 = (bf16[256,2048]{1,0:T(8,128)(2,1)}, bf16[256,2048]{1,0:T(8,128)(2,1)S(1)}, u32[]{:S(2)}, u32[]{:S(2)}) collective-permute-start(bf16[256,2048]{1,0:T(8,128)(2,1)} %get-tuple-element.73.refs_5_), channel_id=1, source_target_pairs={{0,0},{1,4},{2,2},{3,6},{4,1},{5,5},{6,3},{7,7},{8,8},{9,12},{10,1... | collective-permute-start | bytes 3145736 | tf_op jit(solution)/shard_map/ppermute | solution.py:555
  146.6 39.1 %collective-permute-start.28 = (bf16[256,2048]{1,0:T(8,128)(2,1)}, bf16[256,2048]{1,0:T(8,128)(2,1)S(1)}, u32[]{:S(2)}, u32[]{:S(2)}) collective-permute-start(bf16[256,2048]{1,0:T(8,128)(2,1)} %get-tuple-element.74), channel_id=1, source_target_pairs={{0,2},{1,6},{2,0},{3,4},{4,3},{5,7},{6,1},{7,5},{8,10},{9,14},{10,... | collective-permute-start | bytes 3145736 | tf_op jit(solution)/shard_map/ppermute | solution.py:555
  163.8 21.8 %collective-permute-start.32 = (bf16[160,2048]{1,0:T(8,128)(2,1)}, bf16[160,2048]{1,0:T(8,128)(2,1)S(1)}, u32[]{:S(2)}, u32[]{:S(2)}) collective-permute-start(bf16[160,2048]{1,0:T(8,128)(2,1)} %get-tuple-element.78), channel_id=1, source_target_pairs={{0,2},{1,6},{2,0},{3,4},{4,3},{5,7},{6,1},{7,5},{8,10},{9,14},{10,... | collective-permute-start | bytes 1966088 | tf_op jit(solution)/shard_map/ppermute | solution.py:555
  186.6 4.2 %collective-permute-start.33 = (bf16[288,2048]{1,0:T(8,128)(2,1)S(1)}, bf16[288,2048]{1,0:T(8,128)(2,1)S(1)}, u32[]{:S(2)}, u32[]{:S(2)}) collective-permute-start(bf16[288,2048]{1,0:T(8,128)(2,1)S(1)} %get-tuple-element.80.refs_1_), channel_id=1, source_target_pairs={{0,1},{1,0},{2,3},{3,2},{4,5},{5,4},{6,7},{7,6},{8,9},{9,8},{10,11... | collective-permute-start | bytes 3538952 | tf_op jit(solution)/shard_map/ppermute | solution.py:555
  (21 other events, 191.9 us)

commit v2 on v1

--- a/solution.py
+++ b/solution.py
@@ -47,12 +47,12 @@
 COST = pl.CostEstimate(flops=0, bytes_accessed=0, transcendentals=0)
 
 
-def call(kernel, out_shape, in_specs, name, scratch=(), mib=20):
+def call(kernel, out_shape, in_specs, name, scratch=(), mib=20, out_spec=VMEM):
     return pl.pallas_call(
         kernel,
         out_shape=out_shape,
         in_specs=in_specs,
-        out_specs=jax.tree.map(lambda _: VMEM, out_shape),
+        out_specs=jax.tree.map(lambda _: out_spec, out_shape),
         scratch_shapes=scratch,
         compiler_params=params(mib),
         cost_estimate=COST,
@@ -458,16 +458,23 @@
 
 def neighbour_kernel(place, *refs):
     mine, other, w_key, w_value = refs[:4]
-    terms, (whole, key_room, value_room, sems) = refs[4:-4], refs[-4:]
+    terms, rooms = refs[4:-6], refs[-6:]
+    whole, key_room, value_room, sems, term_room, term_sems = rooms
     cols = terms[0].shape[1]
     where = [place[1 + piece] for piece in range(len(terms))]
     wait, places = load_pair(where, cols, w_key, w_value, key_room, value_room, sems)
     set_halves(place[0], mine, other, whole)
+    copies = []
     for i, (piece, there, room) in enumerate(places):
         wait(2 * i)
         wait(2 * i + 1)
         term = contract(whole[0], key_room[room]) + contract(whole[1], value_room[room])
-        terms[piece][:, there] = term.astype(jnp.bfloat16)
+        term_room[:, room] = term.astype(jnp.bfloat16)
+        target = terms[piece].at[:, there]
+        copies.append(pltpu.make_async_copy(term_room.at[:, room], target, term_sems.at[i]))
+        copies[-1].start()
+    for copy in copies:
+        copy.wait()
 
 
 def neighbour_terms(core, chips, mine, other, w_key, w_value, cols):
@@ -478,8 +485,14 @@
         (jax.ShapeDtypeStruct((n_keys, cols), jnp.bfloat16),) * chips.shape[0],
         [SMEM, VMEM, VMEM, HBM, HBM],
         "neighbour_terms",
-        (pltpu.VMEM((2, n_keys, width), jnp.bfloat16), *pair_scratch(width, depth, cols)),
+        (
+            pltpu.VMEM((2, n_keys, width), jnp.bfloat16),
+            *pair_scratch(width, depth, cols),
+            pltpu.VMEM((n_keys, depth), jnp.bfloat16),
+            pltpu.SemaphoreType.DMA((depth // min(TILE, cols),)),
+        ),
         54,
+        ANY,
     )(jnp.concatenate([core[None], chips]), mine, other, w_key, w_value)
 
 

time: 194 us -> 194 us (level)
  transfers between devices with their start and end apart: 34 -> 34, of which waited for: 13 -> 14; matrix products, arithmetic and copies ran while one was open for 14% -> 14% of each run, Pallas kernels for 15% -> 16%
where the time goes in v2:
time: 194 us; the launch traced here: 192 us
  Pallas kernels  53.9 us (28%)
  waiting for transfers between devices  53.8 us (28%)
  starting transfers between devices  47.2 us (24%)
  local copies, waits for them, and re-layouts  27.6 us (14%)
  other arithmetic  8.43 us (4%)
    ppermute x34, waiting for transfers between devices, move(): return lax.ppermute(array, AXES, pairs)  53.8 us
    ppermute x34, starting transfers between devices, move(): return lax.ppermute(array, AXES, pairs)  47.2 us
    gather x4, local copies, waits for them, and re-layouts, look_up(): embed_table.at[wanted[step].reshape(-1)].get(mode='promise_in_bounds')  17.9 us
    pallas_call x1, Pallas kernels, token_terms(): call(token_kernel, (jax.ShapeDtypeStruct((2 * used, cols), jnp.bfloat16),...  9.88 us
    pallas_call x1, Pallas kernels, neighbour_terms(): call(neighbour_kernel, (jax.ShapeDtypeStruct((n_keys, cols), jnp.bfloat16...  9.61 us
    pallas_call x1, Pallas kernels, directions(): call(direction_kernel, (jax.ShapeDtypeStruct((2 * width // HD, cols), jnp...  8.4 us
    unnamed x22, local copies, waits for them, and re-layouts  8.26 us
    pallas_call x1, Pallas kernels, query_sums(): call(lambda *refs: query_kernel(len(tokens), *refs), jax.ShapeDtypeStruct...  7.02 us
  transfers between devices with their start and end apart: 34, of which 14 were waited for; matrix products, arithmetic and copies ran while one was open for 14% of the time, Pallas kernels for 16%

profile of v2, /device:TPU:0, one launch (start us, length us, event | category | flops | bytes accessed | tf_op | source)
XLA Modules:
  0.0 192.2 jit_solution(16929086223328495097)
XLA Ops:
  3.0 5.0 %collective-permute-start.3 = (s32[2,256]{1,0:T(2,128)S(1)}, s32[2,256]{1,0:T(2,128)S(1)}, u32[]{:S(2)}, u32[]{:S(2)}) collective-permute-start(s32[2,256]{1,0:T(2,128)S(1)} %get-tuple-element.99), channel_id=1, source_target_pairs={{0,24},{1,25},{2,26},{3,27},{4,28},{5,29},{6,30},{7,31},{8,16},{9,... | collective-permute-start | bytes 6152 | tf_op jit(solution)/shard_map/ppermute | solution.py:568
  13.7 4.4 %gather_fusion = bf16[128,2048]{1,0:T(8,128)(2,1)} fusion(bf16[8192,2048]{1,0:T(8,128)(2,1)} %param.12, s32[1024]{0:T(1024)S(1)} %pad_clamp_fusion.3), kind=kCustom, calls=%fused_computation | custom fusion | bytes 1049088 | tf_op jit(solution)/shard_map/gather | solution.py:613
  18.2 4.9 %collective-permute-start.4 = (bf16[128,2048]{1,0:T(8,128)(2,1)}, bf16[128,2048]{1,0:T(8,128)(2,1)S(1)}, u32[]{:S(2)}, u32[]{:S(2)}) collective-permute-start(bf16[128,2048]{1,0:T(8,128)(2,1)} %gather_fusion), channel_id=1, source_target_pairs={{0,24},{1,25},{2,26},{3,27},{4,28},{5,29},{6,30},{7,31},{8,16},{9,... | collective-permute-start | bytes 1572872 | tf_op jit(solution)/shard_map/ppermute | solution.py:568
  23.1 4.4 %gather_fusion.1 = bf16[128,2048]{1,0:T(8,128)(2,1)} fusion(bf16[8192,2048]{1,0:T(8,128)(2,1)} %param.12, s32[1024]{0:T(1024)S(1)} %pad_clamp_fusion.2), kind=kCustom, calls=%fused_computation.1 | custom fusion | bytes 1049088 | tf_op jit(solution)/shard_map/gather | solution.py:613
  27.6 5.6 %gather_fusion.2 = bf16[128,2048]{1,0:T(8,128)(2,1)} fusion(bf16[8192,2048]{1,0:T(8,128)(2,1)} %param.12, s32[1024]{0:T(1024)S(1)} %pad_clamp_fusion.1), kind=kCustom, calls=%fused_computation.2 | custom fusion | bytes 1049088 | tf_op jit(solution)/shard_map/gather | solution.py:613
  33.2 7.0 %query_sums.1 = f32[160,1024]{1,0:T(8,128)S(1)} custom-call(s32[2]{0:T(128)S(1)} %iota_xor_fusion.refs_0_.chips, bf16[160,2048]{1,0:T(8,128)(2,1)S(1)} %collective-permute-done.5.refs_1_, bf16[160,2048]{1,0:T(8,128)(2,1)S(1)} %collective-permute-done.6.refs_2_, bf16[4096,1024]{1,0:T(8,128)(2,1)} %refs_4_.3, bf16[1024,4096]{1,0:T(8,128)(2,1)} %refs_3_.5), custom_call_target="tpu_custom_call" | custom-call | tf_op jit(solution)/shard_map/query_sums/pallas_call | solution.py:136
  40.2 3.4 %collective-permute-start.13 = (f32[160,1024]{1,0:T(8,128)S(1)}, f32[160,1024]{1,0:T(8,128)S(1)}, u32[]{:S(2)}, u32[]{:S(2)}) collective-permute-start(f32[160,1024]{1,0:T(8,128)S(1)} %query_sums.1), channel_id=1, source_target_pairs={{0,1},{1,0},{2,3},{3,2},{4,5},{5,4},{6,7},{7,6},{8,9},{9,8},{10,11... | collective-permute-start | bytes 1966088 | tf_op jit(solution)/shard_map/ppermute | solution.py:568
  44.0 3.5 %gather_fusion.3 = bf16[128,2048]{1,0:T(8,128)(2,1)} fusion(bf16[8192,2048]{1,0:T(8,128)(2,1)} %param.12, s32[1024]{0:T(1024)S(1)} %pad_clamp_fusion), kind=kCustom, calls=%fused_computation.3 | custom fusion | bytes 1049088 | tf_op jit(solution)/shard_map/gather | solution.py:613
  47.5 5.2 %collective-permute-start.8 = (bf16[128,2048]{1,0:T(8,128)(2,1)}, bf16[128,2048]{1,0:T(8,128)(2,1)S(1)}, u32[]{:S(2)}, u32[]{:S(2)}) collective-permute-start(bf16[128,2048]{1,0:T(8,128)(2,1)} %gather_fusion.2), channel_id=1, source_target_pairs={{0,8},{1,9},{2,10},{3,11},{4,12},{5,13},{6,14},{7,15},{8,0},{9,1},... | collective-permute-start | bytes 1572872 | tf_op jit(solution)/shard_map/ppermute | solution.py:568
  53.5 8.4 %directions.1 = (bf16[16,2048]{1,0:T(8,128)(2,1)}, bf16[16,2048]{1,0:T(8,128)(2,1)}) custom-call(s32[2]{0:T(128)} %copy-done.6, f32[2,1024]{1,0:T(2,128)} %maximum_convert_fusion.last, bf16[4096,1024]{1,0:T(8,128)(2,1)} %refs_2_.1, bf16[4096,1024]{1,0:T(8,128)(2,1)} %refs_3_.4, bf16[128,2048]{1,0:T(8,128)(2,1)} %gather_fusion.3), custom_call_target="tpu_custom_call" | custom-call | tf_op jit(solution)/shard_map/directions/pallas_call | solution.py:171
  65.0 9.6 %collective-permute-done.8.refs_2_ = bf16[128,2048]{1,0:T(8,128)(2,1)S(1)} collective-permute-done((bf16[128,2048]{1,0:T(8,128)(2,1)}, bf16[128,2048]{1,0:T(8,128)(2,1)S(1)}, u32[]{:S(2)}, u32[]{:S(2)}) %collective-permute-start.8) | collective-permute-done | bytes 524320 | tf_op jit(solution)/shard_map/ppermute | solution.py:568
  74.6 2.1 %collective-permute-start.14 = (bf16[16,2048]{1,0:T(8,128)(2,1)}, bf16[16,2048]{1,0:T(8,128)(2,1)}, u32[]{:S(2)}, u32[]{:S(2)}) collective-permute-start(bf16[16,2048]{1,0:T(8,128)(2,1)} %get-tuple-element.57), channel_id=1, source_target_pairs={{0,0},{1,4},{2,2},{3,6},{4,1},{5,5},{6,3},{7,7},{8,8},{9,12},{10,1... | collective-permute-start | bytes 196616 | tf_op jit(solution)/shard_map/ppermute | solution.py:568
  82.8 2.3 %settle.1 = (bf16[256,2048]{1,0:T(8,128)(2,1)S(1)}, bf16[256,2048]{1,0:T(8,128)(2,1)S(1)}) custom-call(bf16[2,256,512]{2,1,0:T(8,128)(2,1)S(1)} %copy.43.place, bf16[128,2048]{1,0:T(8,128)(2,1)S(1)} %copy-done.2, bf16[128,2048]{1,0:T(8,128)(2,1)S(1)} %collective-permute-done.7.refs_1_, bf16[128,2048]{1,0:T(8,128)(2,1)S(1)} %collective-permute-done.8.refs_2_, ...), custom_call_target="tpu_custom_call" | custom-call | tf_op jit(solution)/shard_map/settle/pallas_call | solution.py:195
  86.7 2.4 %collective-permute-start.20 = (f32[64,256]{1,0:T(8,128)S(1)}, f32[64,256]{1,0:T(8,128)S(1)}, u32[]{:S(2)}, u32[]{:S(2)}) collective-permute-start(f32[64,256]{1,0:T(8,128)S(1)} %scores_along.1.refs_1_), channel_id=1, source_target_pairs={{0,6},{1,7},{2,4},{3,5},{4,2},{5,3},{6,0},{7,1},{8,14},{9,15},{10,... | collective-permute-start | bytes 196616 | tf_op jit(solution)/shard_map/ppermute | solution.py:568
  98.1 3.4 %copy-done = bf16[4096,1024]{1,0:T(8,128)(2,1)S(1)} copy-done((bf16[4096,1024]{1,0:T(8,128)(2,1)S(1)}, bf16[4096,1024]{1,0:T(8,128)(2,1)}, u32[]{:S(2)}) %copy-start) | copy-done | bytes 8388632
  101.5 3.4 %copy-done.1 = bf16[4096,1024]{1,0:T(8,128)(2,1)S(1)} copy-done((bf16[4096,1024]{1,0:T(8,128)(2,1)S(1)}, bf16[4096,1024]{1,0:T(8,128)(2,1)}, u32[]{:S(2)}) %copy-start.1) | copy-done | bytes 8388632
  106.0 12.5 %collective-permute-done.24.refs_4_ = bf16[16,2048]{1,0:T(8,128)(2,1)S(1)} collective-permute-done((bf16[16,2048]{1,0:T(8,128)(2,1)S(1)}, bf16[16,2048]{1,0:T(8,128)(2,1)S(1)}, u32[]{:S(2)}, u32[]{:S(2)}) %collective-permute-start.24) | collective-permute-done | bytes 65568 | tf_op jit(solution)/shard_map/ppermute | solution.py:568
  118.5 5.5 %project.1 = (f32[2,256,512]{2,1,0:T(8,128)S(1)}, f32[2,256,512]{2,1,0:T(8,128)S(1)}, f32[2,16,1024]{2,1,0:T(8,128)S(1)}) custom-call(s32[3]{0:T(128)S(1)} %pad_add_fusion.refs_0_.place, bf16[256,2048]{1,0:T(8,128)(2,1)S(1)} %collective-permute-done.21.refs_1_, bf16[16,2048]{1,0:T(8,128)(2,1)S(1)} %collective-permute-done.22.refs_2_, ...), custom_call_target="tpu_custom_call" | custom-call | tf_op jit(solution)/shard_map/project/pallas_call | solution.py:389
  128.3 3.1 %attend.1 = (bf16[2,256,512]{2,1,0:T(8,128)(2,1)S(1)}, bf16[2,80,512]{2,1,0:T(8,128)(2,1)S(1)}) custom-call(s32[2]{0:T(128)S(1)} %pad_add_fusion.1.place, f32[2,256,512]{2,1,0:T(8,128)S(1)} %get-tuple-element.70.mine, f32[2,256,512]{2,1,0:T(8,128)S(1)} %collective-permute-done.25.other, bf16[80,1024]{1,0:T(8,128)(2,1)S(1)} %get-tuple-element.101.query, ...), custom_call_target="tpu_custom_call" | custom-call | tf_op jit(solution)/shard_map/attend/pallas_call | solution.py:438
  134.2 9.6 %neighbour_terms.1 = (bf16[256,2048]{1,0:T(8,128)(2,1)}, bf16[256,2048]{1,0:T(8,128)(2,1)}) custom-call(s32[3]{0:T(128)} %copy-done.5, bf16[2,256,512]{2,1,0:T(8,128)(2,1)} %copy-done.3, bf16[2,256,512]{2,1,0:T(8,128)(2,1)} %copy-done.8, bf16[4096,1024]{1,0:T(8,128)(2,1)} %refs_2_.1, bf16[4096,1024]{1,0:T(8,128)(2,1)} %refs_3_.4), custom_call_target="tpu_custom_call" | custom-call | tf_op jit(solution)/shard_map/neighbour_terms/pallas_call | solution.py:483
  151.3 9.9 %token_terms.1 = (bf16[160,2048]{1,0:T(8,128)(2,1)}, bf16[160,2048]{1,0:T(8,128)(2,1)}) custom-call(s32[3]{0:T(128)} %copy-done.5, bf16[2,80,512]{2,1,0:T(8,128)(2,1)} %copy-done.4, bf16[2,80,512]{2,1,0:T(8,128)(2,1)} %copy-done.9, f32[2,1024]{1,0:T(2,128)} %fusion.19.refs_2_, bf16[1024,4096]{1,0:T(8,128)(2,1)} %refs_3_.5, bf16[4096,1024]{1,0:T(8,128)(2,1)} %refs_4_.3, ...), custom_call_target="tpu_custom_call" | custom-call | tf_op jit(solution)/shard_map/token_terms/pallas_call | solution.py:529
  163.5 21.3 %collective-permute-done.32.refs_4_ = bf16[160,2048]{1,0:T(8,128)(2,1)S(1)} collective-permute-done((bf16[160,2048]{1,0:T(8,128)(2,1)}, bf16[160,2048]{1,0:T(8,128)(2,1)S(1)}, u32[]{:S(2)}, u32[]{:S(2)}) %collective-permute-start.32) | collective-permute-done | bytes 655392 | tf_op jit(solution)/shard_map/ppermute | solution.py:568
  187.4 2.1 %second_grads.1.refs_3_ = f32[2,128,2048]{2,1,0:T(8,128)} custom-call(s32[1]{0:T(128)} %bitcast.refs_0_.core, f32[64,256]{1,0:T(8,128)S(1)} %get-tuple-element.81.mixed, bf16[64,2048]{1,0:T(8,128)(2,1)S(1)} %bitcast.64), custom_call_target="tpu_custom_call" | custom-call | tf_op jit(solution)/shard_map/second_grads/pallas_call | solution.py:330
  189.9 2.3 %finish.1 = (f32[2,128,2048]{2,1,0:T(8,128)}, f32[128,2048]{1,0:T(8,128)}, f32[128,2048]{1,0:T(8,128)}) custom-call(f32[128,2048]{1,0:T(8,128)S(1)} %get-tuple-element.79.refs_0_, bf16[288,2048]{1,0:T(8,128)(2,1)S(1)} %get-tuple-element.80.refs_1_, bf16[288,2048]{1,0:T(8,128)(2,1)S(1)} %collective-permute-done.33.refs_2_, ...), custom_call_target="tpu_custom_call", output_to_operand_aliasing={{0}: (3, {})} | custom-call | tf_op jit(solution)/shard_map/finish/pallas_call | solution.py:258
  (142 shorter events, 50.0 us)
Async XLA Ops:
  3.0 10.2 %collective-permute-start.3 = (s32[2,256]{1,0:T(2,128)S(1)}, s32[2,256]{1,0:T(2,128)S(1)}, u32[]{:S(2)}, u32[]{:S(2)}) collective-permute-start(s32[2,256]{1,0:T(2,128)S(1)} %get-tuple-element.99), channel_id=1, source_target_pairs={{0,24},{1,25},{2,26},{3,27},{4,28},{5,29},{6,30},{7,31},{8,16},{9,... | collective-permute-start | bytes 6152 | tf_op jit(solution)/shard_map/ppermute | solution.py:568
  7.9 5.1 %collective-permute-start.2 = (s32[2,256]{1,0:T(2,128)S(1)}, s32[2,256]{1,0:T(2,128)S(1)}, u32[]{:S(2)}, u32[]{:S(2)}) collective-permute-start(s32[2,256]{1,0:T(2,128)S(1)} %get-tuple-element.99), channel_id=1, source_target_pairs={{0,16},{1,17},{2,18},{3,19},{4,20},{5,21},{6,22},{7,23},{8,24},{9,... | collective-permute-start | bytes 6152 | tf_op jit(solution)/shard_map/ppermute | solution.py:568
  7.9 5.1 %collective-permute-start.1 = (s32[2,256]{1,0:T(2,128)S(1)}, s32[2,256]{1,0:T(2,128)S(1)}, u32[]{:S(2)}, u32[]{:S(2)}) collective-permute-start(s32[2,256]{1,0:T(2,128)S(1)} %get-tuple-element.99), channel_id=1, source_target_pairs={{0,8},{1,9},{2,10},{3,11},{4,12},{5,13},{6,14},{7,15},{8,0},{9,1},... | collective-permute-start | bytes 6152 | tf_op jit(solution)/shard_map/ppermute | solution.py:568
  9.8 23.4 %collective-permute-start.5 = (bf16[160,2048]{1,0:T(8,128)(2,1)S(1)}, bf16[160,2048]{1,0:T(8,128)(2,1)S(1)}, u32[]{:S(2)}, u32[]{:S(2)}) collective-permute-start(bf16[160,2048]{1,0:T(8,128)(2,1)S(1)} %pad_maximum_fusion), channel_id=1, source_target_pairs={{0,0},{1,4},{2,2},{3,6},{4,1},{5,5},{6,3},{7,7},{8,8},{9,12},{10,1... | collective-permute-start | bytes 1966088 | tf_op jit(solution)/shard_map/ppermute | solution.py:568
  10.5 22.7 %collective-permute-start.6 = (bf16[160,2048]{1,0:T(8,128)(2,1)S(1)}, bf16[160,2048]{1,0:T(8,128)(2,1)S(1)}, u32[]{:S(2)}, u32[]{:S(2)}) collective-permute-start(bf16[160,2048]{1,0:T(8,128)(2,1)S(1)} %pad_maximum_fusion), channel_id=1, source_target_pairs={{0,2},{1,6},{2,0},{3,4},{4,3},{5,7},{6,1},{7,5},{8,10},{9,14},{10,... | collective-permute-start | bytes 1966088 | tf_op jit(solution)/shard_map/ppermute | solution.py:568
  18.2 22.1 %collective-permute-start.4 = (bf16[128,2048]{1,0:T(8,128)(2,1)}, bf16[128,2048]{1,0:T(8,128)(2,1)S(1)}, u32[]{:S(2)}, u32[]{:S(2)}) collective-permute-start(bf16[128,2048]{1,0:T(8,128)(2,1)} %gather_fusion), channel_id=1, source_target_pairs={{0,24},{1,25},{2,26},{3,27},{4,28},{5,29},{6,30},{7,31},{8,16},{9,... | collective-permute-start | bytes 1572872 | tf_op jit(solution)/shard_map/ppermute | solution.py:568
  40.2 12.5 %collective-permute-start.13 = (f32[160,1024]{1,0:T(8,128)S(1)}, f32[160,1024]{1,0:T(8,128)S(1)}, u32[]{:S(2)}, u32[]{:S(2)}) collective-permute-start(f32[160,1024]{1,0:T(8,128)S(1)} %query_sums.1), channel_id=1, source_target_pairs={{0,1},{1,0},{2,3},{3,2},{4,5},{5,4},{6,7},{7,6},{8,9},{9,8},{10,11... | collective-permute-start | bytes 1966088 | tf_op jit(solution)/shard_map/ppermute | solution.py:568
  47.5 27.1 %collective-permute-start.8 = (bf16[128,2048]{1,0:T(8,128)(2,1)}, bf16[128,2048]{1,0:T(8,128)(2,1)S(1)}, u32[]{:S(2)}, u32[]{:S(2)}) collective-permute-start(bf16[128,2048]{1,0:T(8,128)(2,1)} %gather_fusion.2), channel_id=1, source_target_pairs={{0,8},{1,9},{2,10},{3,11},{4,12},{5,13},{6,14},{7,15},{8,0},{9,1},... | collective-permute-start | bytes 1572872 | tf_op jit(solution)/shard_map/ppermute | solution.py:568
  52.7 25.9 %collective-permute-start.10 = (bf16[128,2048]{1,0:T(8,128)(2,1)}, bf16[128,2048]{1,0:T(8,128)(2,1)S(1)}, u32[]{:S(2)}, u32[]{:S(2)}) collective-permute-start(bf16[128,2048]{1,0:T(8,128)(2,1)} %gather_fusion.1), channel_id=1, source_target_pairs={{0,16},{1,17},{2,18},{3,19},{4,20},{5,21},{6,22},{7,23},{8,24},{9,... | collective-permute-start | bytes 1572872 | tf_op jit(solution)/shard_map/ppermute | solution.py:568
  61.9 16.8 %collective-permute-start.17 = (bf16[16,2048]{1,0:T(8,128)(2,1)}, bf16[16,2048]{1,0:T(8,128)(2,1)S(1)}, u32[]{:S(2)}, u32[]{:S(2)}) collective-permute-start(bf16[16,2048]{1,0:T(8,128)(2,1)} %get-tuple-element.58), channel_id=1, source_target_pairs={{0,3},{1,7},{2,1},{3,5},{4,2},{5,6},{6,0},{7,4},{8,11},{9,15},{10,... | collective-permute-start | bytes 196616 | tf_op jit(solution)/shard_map/ppermute | solution.py:568
  62.0 17.3 %collective-permute-start.15 = (bf16[16,2048]{1,0:T(8,128)(2,1)}, bf16[16,2048]{1,0:T(8,128)(2,1)}, u32[]{:S(2)}, u32[]{:S(2)}) collective-permute-start(bf16[16,2048]{1,0:T(8,128)(2,1)} %get-tuple-element.58), channel_id=1, source_target_pairs={{0,2},{1,6},{2,0},{3,4},{4,3},{5,7},{6,1},{7,5},{8,10},{9,14},{10,... | collective-permute-start | bytes 196616 | tf_op jit(solution)/shard_map/ppermute | solution.py:568
  63.3 15.9 %collective-permute-start.16 = (bf16[16,2048]{1,0:T(8,128)(2,1)}, bf16[16,2048]{1,0:T(8,128)(2,1)}, u32[]{:S(2)}, u32[]{:S(2)}) collective-permute-start(bf16[16,2048]{1,0:T(8,128)(2,1)} %get-tuple-element.57), channel_id=1, source_target_pairs={{0,1},{1,5},{2,3},{3,7},{4,0},{5,4},{6,2},{7,6},{8,9},{9,13},{10,1... | collective-permute-start | bytes 196616 | tf_op jit(solution)/shard_map/ppermute | solution.py:568
  74.6 5.2 %collective-permute-start.14 = (bf16[16,2048]{1,0:T(8,128)(2,1)}, bf16[16,2048]{1,0:T(8,128)(2,1)}, u32[]{:S(2)}, u32[]{:S(2)}) collective-permute-start(bf16[16,2048]{1,0:T(8,128)(2,1)} %get-tuple-element.57), channel_id=1, source_target_pairs={{0,0},{1,4},{2,2},{3,6},{4,1},{5,5},{6,3},{7,7},{8,8},{9,12},{10,1... | collective-permute-start | bytes 196616 | tf_op jit(solution)/shard_map/ppermute | solution.py:568
  85.5 4.5 %collective-permute-start.18 = (f32[64,256]{1,0:T(8,128)S(1)}, f32[64,256]{1,0:T(8,128)S(1)}, u32[]{:S(2)}, u32[]{:S(2)}) collective-permute-start(f32[64,256]{1,0:T(8,128)S(1)} %scores_along.1.refs_1_), channel_id=1, source_target_pairs={{0,2},{1,3},{2,0},{3,1},{4,6},{5,7},{6,4},{7,5},{8,10},{9,11},{10,... | collective-permute-start | bytes 196616 | tf_op jit(solution)/shard_map/ppermute | solution.py:568
  86.1 5.0 %collective-permute-start.19 = (f32[64,256]{1,0:T(8,128)S(1)}, f32[64,256]{1,0:T(8,128)S(1)}, u32[]{:S(2)}, u32[]{:S(2)}) collective-permute-start(f32[64,256]{1,0:T(8,128)S(1)} %scores_along.1.refs_1_), channel_id=1, source_target_pairs={{0,4},{1,5},{2,6},{3,7},{4,0},{5,1},{6,2},{7,3},{8,12},{9,13},{10,... | collective-permute-start | bytes 196616 | tf_op jit(solution)/shard_map/ppermute | solution.py:568
  86.7 5.2 %collective-permute-start.20 = (f32[64,256]{1,0:T(8,128)S(1)}, f32[64,256]{1,0:T(8,128)S(1)}, u32[]{:S(2)}, u32[]{:S(2)}) collective-permute-start(f32[64,256]{1,0:T(8,128)S(1)} %scores_along.1.refs_1_), channel_id=1, source_target_pairs={{0,6},{1,7},{2,4},{3,5},{4,2},{5,3},{6,0},{7,1},{8,14},{9,15},{10,... | collective-permute-start | bytes 196616 | tf_op jit(solution)/shard_map/ppermute | solution.py:568
  91.9 26.6 %collective-permute-start.21 = (bf16[256,2048]{1,0:T(8,128)(2,1)S(1)}, bf16[256,2048]{1,0:T(8,128)(2,1)S(1)}, u32[]{:S(2)}, u32[]{:S(2)}) collective-permute-start(bf16[256,2048]{1,0:T(8,128)(2,1)S(1)} %get-tuple-element.61), channel_id=1, source_target_pairs={{0,0},{1,4},{2,2},{3,6},{4,1},{5,5},{6,3},{7,7},{8,8},{9,12},{10,1... | collective-permute-start | bytes 3145736 | tf_op jit(solution)/shard_map/ppermute | solution.py:568
  92.6 25.9 %collective-permute-start.23 = (bf16[256,2048]{1,0:T(8,128)(2,1)S(1)}, bf16[256,2048]{1,0:T(8,128)(2,1)S(1)}, u32[]{:S(2)}, u32[]{:S(2)}) collective-permute-start(bf16[256,2048]{1,0:T(8,128)(2,1)S(1)} %get-tuple-element.61), channel_id=1, source_target_pairs={{0,2},{1,6},{2,0},{3,4},{4,3},{5,7},{6,1},{7,5},{8,10},{9,14},{10,... | collective-permute-start | bytes 3145736 | tf_op jit(solution)/shard_map/ppermute | solution.py:568
  96.8 9.3 %collective-permute-start.22 = (bf16[16,2048]{1,0:T(8,128)(2,1)S(1)}, bf16[16,2048]{1,0:T(8,128)(2,1)S(1)}, u32[]{:S(2)}, u32[]{:S(2)}) collective-permute-start(bf16[16,2048]{1,0:T(8,128)(2,1)S(1)} %get-tuple-element.66), channel_id=1, source_target_pairs={{0,0},{1,4},{2,2},{3,6},{4,1},{5,5},{6,3},{7,7},{8,8},{9,12},{10,1... | collective-permute-start | bytes 196616 | tf_op jit(solution)/shard_map/ppermute | solution.py:568
  97.4 21.1 %collective-permute-start.24 = (bf16[16,2048]{1,0:T(8,128)(2,1)S(1)}, bf16[16,2048]{1,0:T(8,128)(2,1)S(1)}, u32[]{:S(2)}, u32[]{:S(2)}) collective-permute-start(bf16[16,2048]{1,0:T(8,128)(2,1)S(1)} %get-tuple-element.67), channel_id=1, source_target_pairs={{0,2},{1,6},{2,0},{3,4},{4,3},{5,7},{6,1},{7,5},{8,10},{9,14},{10,... | collective-permute-start | bytes 196616 | tf_op jit(solution)/shard_map/ppermute | solution.py:568
  124.0 4.3 %collective-permute-start.25 = (f32[2,256,512]{2,1,0:T(8,128)S(1)}, f32[2,256,512]{2,1,0:T(8,128)S(1)}, u32[]{:S(2)}, u32[]{:S(2)}) collective-permute-start(f32[2,256,512]{2,1,0:T(8,128)S(1)} %get-tuple-element.71), channel_id=1, source_target_pairs={{0,1},{1,0},{2,3},{3,2},{4,5},{5,4},{6,7},{7,6},{8,9},{9,8},{10,11... | collective-permute-start | bytes 3145736 | tf_op jit(solution)/shard_map/ppermute | solution.py:568
  143.8 40.9 %collective-permute-start.27 = (bf16[256,2048]{1,0:T(8,128)(2,1)}, bf16[256,2048]{1,0:T(8,128)(2,1)S(1)}, u32[]{:S(2)}, u32[]{:S(2)}) collective-permute-start(bf16[256,2048]{1,0:T(8,128)(2,1)} %get-tuple-element.73.refs_5_), channel_id=1, source_target_pairs={{0,0},{1,4},{2,2},{3,6},{4,1},{5,5},{6,3},{7,7},{8,8},{9,12},{10,1... | collective-permute-start | bytes 3145736 | tf_op jit(solution)/shard_map/ppermute | solution.py:568
  145.7 39.1 %collective-permute-start.28 = (bf16[256,2048]{1,0:T(8,128)(2,1)}, bf16[256,2048]{1,0:T(8,128)(2,1)S(1)}, u32[]{:S(2)}, u32[]{:S(2)}) collective-permute-start(bf16[256,2048]{1,0:T(8,128)(2,1)} %get-tuple-element.74), channel_id=1, source_target_pairs={{0,2},{1,6},{2,0},{3,4},{4,3},{5,7},{6,1},{7,5},{8,10},{9,14},{10,... | collective-permute-start | bytes 3145736 | tf_op jit(solution)/shard_map/ppermute | solution.py:568
  162.9 21.8 %collective-permute-start.32 = (bf16[160,2048]{1,0:T(8,128)(2,1)}, bf16[160,2048]{1,0:T(8,128)(2,1)S(1)}, u32[]{:S(2)}, u32[]{:S(2)}) collective-permute-start(bf16[160,2048]{1,0:T(8,128)(2,1)} %get-tuple-element.78), channel_id=1, source_target_pairs={{0,2},{1,6},{2,0},{3,4},{4,3},{5,7},{6,1},{7,5},{8,10},{9,14},{10,... | collective-permute-start | bytes 1966088 | tf_op jit(solution)/shard_map/ppermute | solution.py:568
  (21 other events, 194.3 us)
